TPU v7x, 128 devices: a whole 4x4x4 slice. The times are simulated.
128 devices in a mesh: dp: 4 (over y), seq: 32 (over z, x, core).
Axes of the slice: x: 4, y: 4, z: 4, core: 2. Of those that a mesh axis runs over, the one named last changes fastest.
Arguments:
- first_in: bfloat16 [16384, 1024], P(('dp', 'seq')), may hold values from -6 to 6
- second_in: bfloat16 [16384, 1024], P(('dp', 'seq')), may hold values from -6 to 6
- attn_gain: bfloat16 [1024], P(('dp', 'seq')), may hold values from 0.5 to 1.5
- attn_shift: bfloat16 [1024], P(('dp', 'seq')), may hold values from -3 to 3
- w_joint: bfloat16 [1024, 1024], P(('dp', 'seq')), may hold values from -0.375 to 0.375
- w_value: bfloat16 [1024, 1024], P(('dp', 'seq')), may hold values from -0.1875 to 0.1875
- w_output: bfloat16 [1024, 1024], P(('dp', 'seq')), may hold values from -0.75 to 0.75
- ffn_gain: bfloat16 [1024], P(('dp', 'seq')), may hold values from 0.5 to 1.5
- ffn_shift: bfloat16 [1024], P(('dp', 'seq')), may hold values from -3 to 3
- w_inner: bfloat16 [1024, 4096], P(('dp', 'seq')), may hold values from -0.1875 to 0.1875
- b_inner: bfloat16 [4096], P(('dp', 'seq')), may hold values from -3 to 3
- w_outer: bfloat16 [4096, 1024], P(('dp', 'seq')), may hold values from -0.09375 to 0.09375
- b_outer: bfloat16 [1024], P(('dp', 'seq')), may hold values from -3 to 3
- buckets: int32 [4, 16384, 1], P(None, ('dp', 'seq')), may hold values from 0 to 31; in each aligned block of 128 rows (0 to 127, 128 to 255, ..., all dimensions but the last counted through in order) at most 8 rows name the same one
- cot_first: bfloat16 [16384, 1024], P(('dp', 'seq')), may hold values from -6 to 6
- cot_second: bfloat16 [16384, 1024], P(('dp', 'seq')), may hold values from -6 to 6
Outputs:
- first_out: bfloat16 [16384, 1024], P(('dp', 'seq'))
- second_out: bfloat16 [16384, 1024], P(('dp', 'seq'))
- grad_first: bfloat16 [16384, 1024], P(('dp', 'seq'))
- grad_second: bfloat16 [16384, 1024], P(('dp', 'seq'))
- grad_attn_gain: float32 [1024], P(('dp', 'seq'))
- grad_attn_shift: float32 [1024], P(('dp', 'seq'))
- grad_joint: float32 [1024, 1024], P(('dp', 'seq'))
- grad_value: float32 [1024, 1024], P(('dp', 'seq'))
- grad_output: float32 [1024, 1024], P(('dp', 'seq'))
- grad_ffn_gain: float32 [1024], P(('dp', 'seq'))
- grad_ffn_shift: float32 [1024], P(('dp', 'seq'))
- grad_inner: float32 [1024, 4096], P(('dp', 'seq'))
- grad_b_inner: float32 [4096], P(('dp', 'seq'))
- grad_outer: float32 [4096, 1024], P(('dp', 'seq'))
- grad_b_outer: float32 [1024], P(('dp', 'seq'))
Inputs may be any that keep to these rules, and one draw needn't show every extreme that they name: `buckets`: in each round, among the 128 tokens of one device (aligned blocks of rows), no bucket id appears more than 8 times, and in every draw some bucket appears exactly 8 times in some block.
All inputs are finite; a program needn't handle non-finite values.
Results may differ from a plain program's by a relative error of at most 0.015.
The roundings to bfloat16 on the way count: a program that leaves them out, or rounds other values in their place, can miss the bound.
Values may be sent and summed in bfloat16 or wider, within the bound.
No kernel may reach another device: no remote copies, remote signals or barrier semaphores. Data moves between devices by JAX's collectives and lax.ppermute only.
A program may use at most 192 MiB of HBM per device.

v0:
```python
import jax
import jax.numpy as jnp
from jax import lax
from jax.sharding import PartitionSpec as P

HEADS = 8
HEAD_DIM = 128


EPS_NORM = 1e-05
EPS_KEY = 1e-06
SELF_SCORE = -10000.0
MASKED_SCORE = -1000000000.0


def norm_apply(values, gain, shift):
    row_mean = jnp.mean(values, axis=-1, keepdims=True)
    centered = values - row_mean
    spread = jnp.mean(centered * centered, axis=-1, keepdims=True)
    return centered * lax.rsqrt(spread + EPS_NORM) * gain + shift


def unit_keys(joint_proj):
    shaped = joint_proj.reshape(joint_proj.shape[:-1] + (HEADS, HEAD_DIM))
    inverse_norm = lax.rsqrt(jnp.sum(shaped * shaped, axis=-1, keepdims=True) + EPS_KEY)
    return (shaped * inverse_norm).reshape(joint_proj.shape)


def combine_rounds(outputs, totals):
    weights = jax.nn.softmax(totals, axis=0)
    shaped = outputs.reshape(outputs.shape[:-1] + (HEADS, HEAD_DIM))
    mixed_heads = jnp.sum(weights[..., None] * shaped, axis=0)
    return mixed_heads.reshape(mixed_heads.shape[:-2] + (HEADS * HEAD_DIM,))


def slot_plan(buckets, owners, per_owner):
    chosen = buckets[:, :, 0]
    owner_ids = lax.broadcasted_iota(jnp.int32, (1, 1, owners), 2)
    marks = (chosen[:, :, None] == owner_ids).astype(jnp.int32)
    earlier = jnp.cumsum(marks, axis=1) - marks
    ranking = jnp.sum(earlier * marks, axis=2)
    target = chosen * per_owner + ranking
    slot_ids = lax.broadcasted_iota(jnp.int32, (1, owners * per_owner, 1), 1)
    return (slot_ids == target[:, None, :]).astype(jnp.bfloat16)


def send_shared(plan, rows, owners):
    placed = jnp.einsum("rst,tw->rsw", plan, rows, preferred_element_type=jnp.float32)
    return placed.astype(jnp.bfloat16).reshape(
        plan.shape[0], owners, plan.shape[1] // owners, rows.shape[-1]
    )


def send_rounds(plan, rows, owners):
    placed = jnp.einsum("rst,rtw->rsw", plan, rows, preferred_element_type=jnp.float32)
    return placed.astype(jnp.bfloat16).reshape(
        plan.shape[0], owners, plan.shape[1] // owners, rows.shape[-1]
    )


def take_rounds(plan, pieces):
    flat_rows = pieces.reshape(plan.shape[0], plan.shape[1], pieces.shape[-1])
    return jnp.einsum("rst,rsw->rtw", plan, flat_rows, preferred_element_type=jnp.float32)


def take_summed(plan, pieces):
    flat_rows = pieces.reshape(plan.shape[0], plan.shape[1], pieces.shape[-1])
    return jnp.einsum("rst,rsw->tw", plan, flat_rows, preferred_element_type=jnp.float32)


def slot_masks(valid_rows):
    slot_count = valid_rows.shape[-1]
    row_ids = lax.broadcasted_iota(jnp.int32, (slot_count, slot_count), 0)
    col_ids = lax.broadcasted_iota(jnp.int32, (slot_count, slot_count), 1)
    live = valid_rows > 0.5
    allowed = live[:, :, None] & live[:, None, :] & (col_ids <= row_ids)[None]
    return (allowed[:, None], (row_ids == col_ids)[None, None])


def owner_forward(queries, values, valid):
    rounds_here, owners, per_owner, width = queries.shape
    slot_count = owners * per_owner
    shape4 = (rounds_here, slot_count, HEADS, HEAD_DIM)
    query_rows = queries.reshape(shape4)
    keys_low = unit_keys(
        queries.reshape(rounds_here, slot_count, width).astype(jnp.float32)
    ).astype(jnp.bfloat16)
    key_rows = keys_low.reshape(shape4)
    value_rows = values.reshape(shape4)
    allowed, itself = slot_masks(valid.reshape(rounds_here, slot_count))
    scores = jnp.einsum("rqhd,rkhd->rhqk", query_rows, key_rows, preferred_element_type=jnp.float32)
    scores = jnp.where(itself, SELF_SCORE, jnp.where(allowed, scores, MASKED_SCORE))
    row_peak = jnp.max(scores, axis=-1, keepdims=True)
    exponent = jnp.exp(scores - row_peak)
    row_total = jnp.sum(exponent, axis=-1, keepdims=True)
    probabilities = (exponent / row_total).astype(jnp.bfloat16)
    attended = jnp.einsum(
        "rhqk,rkhd->rqhd", probabilities, value_rows, preferred_element_type=jnp.float32
    )
    log_total = jnp.transpose((row_peak + jnp.log(row_total))[..., 0], (0, 2, 1))
    attended_low = attended.astype(jnp.bfloat16).reshape(rounds_here, owners, per_owner, width)
    totals_low = log_total.astype(jnp.bfloat16).reshape(rounds_here, owners, per_owner, HEADS)
    return (attended_low, totals_low, log_total, keys_low)


def owner_backward(queries, values, valid, keys_low, log_total, grad_attended, grad_totals):
    rounds_here, owners, per_owner, width = queries.shape
    slot_count = owners * per_owner
    shape4 = (rounds_here, slot_count, HEADS, HEAD_DIM)
    query_flat = queries.reshape(rounds_here, slot_count, width)
    query_rows = query_flat.reshape(shape4)
    key_rows = keys_low.reshape(shape4)
    value_rows = values.reshape(shape4)
    grad_rows = grad_attended.reshape(shape4)
    grad_log = jnp.transpose(
        grad_totals.reshape(rounds_here, slot_count, HEADS).astype(jnp.float32), (0, 2, 1)
    )[..., None]
    allowed, itself = slot_masks(valid.reshape(rounds_here, slot_count))
    scores = jnp.einsum("rqhd,rkhd->rhqk", query_rows, key_rows, preferred_element_type=jnp.float32)
    scores = jnp.where(itself, SELF_SCORE, jnp.where(allowed, scores, MASKED_SCORE))
    log_rows = jnp.transpose(log_total, (0, 2, 1))[..., None]
    probabilities = jnp.exp(scores - log_rows)
    grad_probs = jnp.einsum(
        "rqhd,rkhd->rhqk", grad_rows, value_rows, preferred_element_type=jnp.float32
    )
    grad_values = jnp.einsum(
        "rhqk,rqhd->rkhd",
        probabilities.astype(jnp.bfloat16),
        grad_rows,
        preferred_element_type=jnp.float32,
    )
    agreement = jnp.sum(probabilities * grad_probs, axis=-1, keepdims=True)
    grad_scores = probabilities * (grad_probs - agreement + grad_log)
    grad_scores = jnp.where(allowed & jnp.logical_not(itself), grad_scores, 0.0).astype(
        jnp.bfloat16
    )
    grad_direct = jnp.einsum(
        "rhqk,rkhd->rqhd", grad_scores, key_rows, preferred_element_type=jnp.float32
    )
    grad_keys = jnp.einsum(
        "rhqk,rqhd->rkhd", grad_scores, query_rows, preferred_element_type=jnp.float32
    )
    unused_keys, key_pull = jax.vjp(unit_keys, query_flat.astype(jnp.float32))
    grad_queries = (
        grad_direct.reshape(rounds_here, slot_count, width)
        + key_pull(grad_keys.reshape(rounds_here, slot_count, width))[0]
    )
    out_shape = (rounds_here, owners, per_owner, width)
    return (
        grad_queries.astype(jnp.bfloat16).reshape(out_shape),
        grad_values.astype(jnp.bfloat16).reshape(out_shape),
    )


def local(
    first_in,
    second_in,
    attn_gain,
    attn_shift,
    w_joint,
    w_value,
    w_output,
    ffn_gain,
    ffn_shift,
    w_inner,
    b_inner,
    w_outer,
    b_outer,
    buckets,
    cot_first,
    cot_second,
):
    owners = lax.axis_size("seq")
    tokens_here = first_in.shape[0]
    per_owner = 2 * tokens_here // owners
    rounds_all = buckets.shape[0]
    attn_set = (
        lax.all_gather(attn_gain, ("dp", "seq"), axis=0, tiled=True),
        lax.all_gather(attn_shift, ("dp", "seq"), axis=0, tiled=True),
        lax.all_gather(w_joint, ("dp", "seq"), axis=0, tiled=True),
        lax.all_gather(w_value, ("dp", "seq"), axis=0, tiled=True),
        lax.all_gather(w_output, ("dp", "seq"), axis=0, tiled=True),
    )
    gain_attn, shift_attn, joint_full, value_full, output_full = attn_set
    gain_attn_f = gain_attn.astype(jnp.float32)
    shift_attn_f = shift_attn.astype(jnp.float32)
    plan = slot_plan(buckets, owners, per_owner)
    second_f = second_in.astype(jnp.float32)
    normed = norm_apply(second_f, gain_attn_f, shift_attn_f).astype(jnp.bfloat16)
    queries = jnp.dot(normed, joint_full, preferred_element_type=jnp.float32).astype(jnp.bfloat16)
    values_low = jnp.dot(normed, value_full, preferred_element_type=jnp.float32).astype(
        jnp.bfloat16
    )
    valid_slots = (
        jnp.sum(plan.astype(jnp.float32), axis=2)
        .astype(jnp.bfloat16)
        .reshape(rounds_all, owners, per_owner)
    )
    received = (
        lax.all_to_all(
            send_shared(plan, queries, owners), "seq", split_axis=1, concat_axis=1, tiled=True
        ),
        lax.all_to_all(
            send_shared(plan, values_low, owners), "seq", split_axis=1, concat_axis=1, tiled=True
        ),
        lax.all_to_all(valid_slots, "seq", split_axis=1, concat_axis=1, tiled=True),
    )
    recv_queries, recv_values, recv_valid = received
    attended_low, totals_low, log_total, keys_low = owner_forward(
        recv_queries, recv_values, recv_valid
    )
    returned = (
        lax.all_to_all(attended_low, "seq", split_axis=1, concat_axis=1, tiled=True),
        lax.all_to_all(totals_low, "seq", split_axis=1, concat_axis=1, tiled=True),
    )
    outputs_tok = take_rounds(plan, returned[0])
    totals_tok = take_rounds(plan, returned[1])
    mixed_heads = combine_rounds(outputs_tok, totals_tok).astype(jnp.bfloat16)
    first_sum = first_in.astype(jnp.float32) + jnp.dot(
        mixed_heads, output_full, preferred_element_type=jnp.float32
    )
    ffn_set = (
        lax.all_gather(ffn_gain, ("dp", "seq"), axis=0, tiled=True),
        lax.all_gather(ffn_shift, ("dp", "seq"), axis=0, tiled=True),
        lax.all_gather(w_inner, ("dp", "seq"), axis=0, tiled=True),
        lax.all_gather(b_inner, ("dp", "seq"), axis=0, tiled=True),
        lax.all_gather(w_outer, ("dp", "seq"), axis=0, tiled=True),
        lax.all_gather(b_outer, ("dp", "seq"), axis=0, tiled=True),
    )
    gain_ffn, shift_ffn, inner_full, bias_inner, outer_full, bias_outer = ffn_set
    gain_ffn_f = gain_ffn.astype(jnp.float32)
    shift_ffn_f = shift_ffn.astype(jnp.float32)
    ffn_input = norm_apply(first_sum, gain_ffn_f, shift_ffn_f).astype(jnp.bfloat16)
    hidden = jnp.dot(ffn_input, inner_full, preferred_element_type=jnp.float32) + bias_inner.astype(
        jnp.float32
    )
    active = jax.nn.gelu(hidden).astype(jnp.bfloat16)
    second_sum = (
        second_f
        + jnp.dot(active, outer_full, preferred_element_type=jnp.float32)
        + bias_outer.astype(jnp.float32)
    )
    first_out = first_sum.astype(jnp.bfloat16)
    second_out = second_sum.astype(jnp.bfloat16)
    ffn_again = (
        lax.all_gather(ffn_gain, ("dp", "seq"), axis=0, tiled=True),
        lax.all_gather(ffn_shift, ("dp", "seq"), axis=0, tiled=True),
        lax.all_gather(w_inner, ("dp", "seq"), axis=0, tiled=True),
        lax.all_gather(b_inner, ("dp", "seq"), axis=0, tiled=True),
        lax.all_gather(w_outer, ("dp", "seq"), axis=0, tiled=True),
        lax.all_gather(b_outer, ("dp", "seq"), axis=0, tiled=True),
    )
    inner_back = ffn_again[2]
    outer_back = ffn_again[4]
    grad_outer = jnp.einsum("tf,td->fd", active, cot_second, preferred_element_type=jnp.float32)
    grad_b_outer = jnp.sum(cot_second.astype(jnp.float32), axis=0)
    grad_active = jnp.einsum(
        "td,fd->tf", cot_second, outer_back, preferred_element_type=jnp.float32
    )
    unused_gelu, gelu_pull = jax.vjp(jax.nn.gelu, hidden)
    grad_hidden = gelu_pull(grad_active)[0].astype(jnp.bfloat16)
    grad_inner = jnp.einsum("td,tf->df", ffn_input, grad_hidden, preferred_element_type=jnp.float32)
    grad_b_inner = jnp.sum(grad_hidden.astype(jnp.float32), axis=0)
    grad_ffn_input = jnp.einsum(
        "tf,df->td", grad_hidden, inner_back, preferred_element_type=jnp.float32
    )
    unused_norm, ffn_pull = jax.vjp(norm_apply, first_sum, gain_ffn_f, shift_ffn_f)
    grad_first_norm, grad_ffn_gain, grad_ffn_shift = ffn_pull(grad_ffn_input)
    ffn_grads = (
        lax.psum_scatter(grad_ffn_gain, ("dp", "seq"), scatter_dimension=0, tiled=True),
        lax.psum_scatter(grad_ffn_shift, ("dp", "seq"), scatter_dimension=0, tiled=True),
        lax.psum_scatter(grad_inner, ("dp", "seq"), scatter_dimension=0, tiled=True),
        lax.psum_scatter(grad_b_inner, ("dp", "seq"), scatter_dimension=0, tiled=True),
        lax.psum_scatter(grad_outer, ("dp", "seq"), scatter_dimension=0, tiled=True),
        lax.psum_scatter(grad_b_outer, ("dp", "seq"), scatter_dimension=0, tiled=True),
    )
    first_total = cot_first.astype(jnp.float32) + grad_first_norm
    grad_first = first_total.astype(jnp.bfloat16)
    attn_again = (
        lax.all_gather(attn_gain, ("dp", "seq"), axis=0, tiled=True),
        lax.all_gather(attn_shift, ("dp", "seq"), axis=0, tiled=True),
        lax.all_gather(w_joint, ("dp", "seq"), axis=0, tiled=True),
        lax.all_gather(w_value, ("dp", "seq"), axis=0, tiled=True),
        lax.all_gather(w_output, ("dp", "seq"), axis=0, tiled=True),
    )
    joint_back = attn_again[2]
    value_back = attn_again[3]
    output_back = attn_again[4]
    branch_grad = first_total.astype(jnp.bfloat16)
    grad_output = jnp.einsum(
        "td,te->de", mixed_heads, branch_grad, preferred_element_type=jnp.float32
    )
    grad_mixed = jnp.einsum(
        "te,de->td", branch_grad, output_back, preferred_element_type=jnp.float32
    )
    unused_mix, combine_pull = jax.vjp(combine_rounds, outputs_tok, totals_tok)
    grad_round_out, grad_round_total = combine_pull(grad_mixed)
    sent_grads = (
        send_rounds(plan, grad_round_out.astype(jnp.bfloat16), owners),
        send_rounds(plan, grad_round_total.astype(jnp.bfloat16), owners),
    )
    recv_grads = (
        lax.all_to_all(sent_grads[0], "seq", split_axis=1, concat_axis=1, tiled=True),
        lax.all_to_all(sent_grads[1], "seq", split_axis=1, concat_axis=1, tiled=True),
    )
    grad_queries, grad_values = owner_backward(
        recv_queries, recv_values, recv_valid, keys_low, log_total, recv_grads[0], recv_grads[1]
    )
    back_rows = (
        lax.all_to_all(grad_queries, "seq", split_axis=1, concat_axis=1, tiled=True),
        lax.all_to_all(grad_values, "seq", split_axis=1, concat_axis=1, tiled=True),
    )
    grad_joint_rows = take_summed(plan, back_rows[0]).astype(jnp.bfloat16)
    grad_value_rows = take_summed(plan, back_rows[1]).astype(jnp.bfloat16)
    grad_joint = jnp.einsum(
        "td,te->de", normed, grad_joint_rows, preferred_element_type=jnp.float32
    )
    grad_value = jnp.einsum(
        "td,te->de", normed, grad_value_rows, preferred_element_type=jnp.float32
    )
    grad_normed = jnp.einsum(
        "te,de->td", grad_joint_rows, joint_back, preferred_element_type=jnp.float32
    )
    grad_normed = grad_normed + jnp.einsum(
        "te,de->td", grad_value_rows, value_back, preferred_element_type=jnp.float32
    )
    unused_attn, attn_pull = jax.vjp(norm_apply, second_f, gain_attn_f, shift_attn_f)
    grad_second_norm, grad_attn_gain, grad_attn_shift = attn_pull(grad_normed)
    attn_grads = (
        lax.psum_scatter(grad_attn_gain, ("dp", "seq"), scatter_dimension=0, tiled=True),
        lax.psum_scatter(grad_attn_shift, ("dp", "seq"), scatter_dimension=0, tiled=True),
        lax.psum_scatter(grad_joint, ("dp", "seq"), scatter_dimension=0, tiled=True),
        lax.psum_scatter(grad_value, ("dp", "seq"), scatter_dimension=0, tiled=True),
        lax.psum_scatter(grad_output, ("dp", "seq"), scatter_dimension=0, tiled=True),
    )
    grad_second = (cot_second.astype(jnp.float32) + grad_second_norm).astype(jnp.bfloat16)
    return (
        first_out,
        second_out,
        grad_first,
        grad_second,
        attn_grads[0],
        attn_grads[1],
        attn_grads[2],
        attn_grads[3],
        attn_grads[4],
        ffn_grads[0],
        ffn_grads[1],
        ffn_grads[2],
        ffn_grads[3],
        ffn_grads[4],
        ffn_grads[5],
    )


def solution(mesh):
    placed = (
        P(("dp", "seq"), None),
        P(("dp", "seq"), None),
        P(("dp", "seq")),
        P(("dp", "seq")),
        P(("dp", "seq"), None),
        P(("dp", "seq"), None),
        P(("dp", "seq"), None),
        P(("dp", "seq")),
        P(("dp", "seq")),
        P(("dp", "seq"), None),
        P(("dp", "seq")),
        P(("dp", "seq"), None),
        P(("dp", "seq")),
        P(None, ("dp", "seq"), None),
        P(("dp", "seq"), None),
        P(("dp", "seq"), None),
    )
    return jax.shard_map(
        local,
        mesh=mesh,
        in_specs=placed,
        out_specs=(
            P(("dp", "seq"), None),
            P(("dp", "seq"), None),
            P(("dp", "seq"), None),
            P(("dp", "seq"), None),
            P(("dp", "seq")),
            P(("dp", "seq")),
            P(("dp", "seq"), None),
            P(("dp", "seq"), None),
            P(("dp", "seq"), None),
            P(("dp", "seq")),
            P(("dp", "seq")),
            P(("dp", "seq"), None),
            P(("dp", "seq")),
            P(("dp", "seq"), None),
            P(("dp", "seq")),
        ),
        check_vma=False,
    )
```

profile of v0, /device:TPU:0, one launch (start us, length us, event | category | flops | bytes accessed | tf_op | source)
XLA Modules:
  0.0 3664.9 jit_solution(9249036967222496784)
XLA Ops:
  14.2 8.2 all-to-all-start
  27.5 68.5 %all-reduce.13 = (bf16[1024]{0:T(1024)(128)(2,1)S(1)}, bf16[1024]{0:T(1024)(128)(2,1)S(1)}, bf16[1024]{0:T(1024)(128)(2,1)}, bf16[4096]{0:T(1024)(128)(2,1)S(1)}...) all-reduce(bf16[1024]{0:T(1024)(128)(2,1)S(1)} %dynamic-update-slic, ...), channel_id=1, replica_groups=mesh['dp'=4,'seq'=32] {'dp','seq'}, use_global_device_ids=true, to_apply=%add.1 | all-reduce | flops 9216 | bytes 36864
  98.3 2.6 convert_bitcast_fusion.3
  102.6 4.0 all-to-all-start.3
  106.6 50.6 %all-gather.6.cloned.1.call-done = bf16[1024,1024]{1,0:T(8,128)(2,1)} async-done(((bf16[8,1024]{1,0:T(8,128)(2,1)}), bf16[1024,1024]{1,0:T(8,128)(2,1)}) %all-gather.6.cloned.1.call-update) | async-done | bytes 2097168 | tf_op jit(solution)/shard_map/all_gather | solution.py:180
  157.1 3.9 convert_bitcast_fusion.4
  161.1 3.1 copy.116
  164.2 5.0 all-to-all-start.1
  172.8 26.5 all-to-all-done.1
  203.0 3.0 copy.118
  214.1 3.8 all-to-all-start.2
  218.0 7.4 convert_bitcast_fusion.2
  225.3 3.1 copy.130
  230.8 3.2 copy.131
  233.9 7.5 all-to-all-start.4
  247.4 24.8 all-to-all-done.4
  272.2 3.6 multiply_reduce_fusion.1
  279.8 36.1 all-gather.14.cloned.1.call-done
  315.9 7.6 fusion.140
  323.5 62.9 %all-gather.12.cloned.1.call-done = bf16[1024,4096]{1,0:T(8,128)(2,1)} async-done(((bf16[8,4096]{1,0:T(8,128)(2,1)}), bf16[1024,4096]{1,0:T(8,128)(2,1)}) %all-gather.12.cloned.1.call-update) | async-done | bytes 8388624 | tf_op jit(solution)/shard_map/all_gather | solution.py:225
  386.5 9.1 convert_reduce_fusion
  395.6 3.6 multiply_reduce_fusion.2
  400.3 2.6 fusion.143
  403.2 2.5 fusion.141
  406.8 34.2 all_to_all.45
  441.8 2.6 copy.150
  444.4 7.7 convert_bitcast_fusion
  452.2 3.1 copy.152
  455.3 2.3 reshape.282
  459.4 32.7 all_to_all.46
  493.3 2.8 fusion.125
  500.0 11.0 all_to_all.47
  512.2 6.8 fusion.57
  519.0 18.1 fusion.16
  537.2 18.2 fusion.13
  555.4 3.1 copy.147
  558.5 2.3 convert_element_type.187
  562.6 32.6 all_to_all.48
  595.9 2.9 fusion.127
  600.4 8.1 fusion.124
  609.7 8.2 fusion.123
  619.5 5.8 fusion.66
  629.3 65.2 %all-reduce.12 = (f32[1024]{0:T(1024)S(1)}, f32[1024]{0:T(1024)S(1)}, f32[1024]{0:T(1024)S(1)}, f32[1024]{0:T(1024)S(1)}, f32[4096]{0:T(1024)S(1)}, /*index=5*/f32[1024]{0:T(1024)S(1)}) all-reduce(f32[1024]{0:T(1024)S(1)} %get-tuple-element.17, f32[1024]{0:T(1024)S(1)} %get-tuple-element.20, ...), channel_id=2, replica_groups=mesh['dp'=4,'seq'=32] {'dp','seq'}, use_global_device_ids=true, to_apply=%region_22.23.clone | all-reduce | flops 9216 | bytes 73728
  698.0 357.1 %reduce-scatter.10.cloned.1.call-done = f32[8,1024]{1,0:T(8,128)} async-done(((f32[1024,1024]{1,0:T(8,128)}), f32[8,1024]{1,0:T(8,128)}) %reduce-scatter.10.cloned.1.call-update) | async-done | bytes 32784 | tf_op jit(solution)/shard_map/reduce_scatter | solution.py:334
  1055.1 639.6 %reduce-scatter.8.cloned.1.call-done = f32[8,1024]{1,0:T(8,128)} async-done(((f32[1024,1024]{1,0:T(8,128)}), f32[8,1024]{1,0:T(8,128)}) %reduce-scatter.8.cloned.1.call-update) | async-done | bytes 32784 | tf_op jit(solution)/shard_map/reduce_scatter | solution.py:333
  1694.7 639.2 %reduce-scatter.6.cloned.1.call-done = f32[8,1024]{1,0:T(8,128)} async-done(((f32[1024,1024]{1,0:T(8,128)}), f32[8,1024]{1,0:T(8,128)}) %reduce-scatter.6.cloned.1.call-update) | async-done | bytes 32784 | tf_op jit(solution)/shard_map/reduce_scatter | solution.py:332
  2333.9 661.9 %reduce-scatter.14.cloned.1.call-done = f32[32,1024]{1,0:T(8,128)} async-done(((f32[4096,1024]{1,0:T(8,128)}), f32[32,1024]{1,0:T(8,128)}) %reduce-scatter.14.cloned.1.call-update) | async-done | bytes 131088 | tf_op jit(solution)/shard_map/reduce_scatter | solution.py:274
  2995.8 661.8 %reduce-scatter.12.cloned.1.call-done = f32[8,4096]{1,0:T(8,128)} async-done(((f32[1024,4096]{1,0:T(8,128)}), f32[8,4096]{1,0:T(8,128)}) %reduce-scatter.12.cloned.1.call-update) | async-done | bytes 131088 | tf_op jit(solution)/shard_map/reduce_scatter | solution.py:272
  (210 shorter events, 68.6 us)
Async XLA Ops:
  7.2 91.1 %copy-start = (bf16[128,1024]{1,0:T(8,128)(2,1)S(1)}, bf16[128,1024]{1,0:T(8,128)(2,1)}, u32[]{:S(2)}) copy-start(bf16[128,1024]{1,0:T(8,128)(2,1)} %param.17) | copy-start | bytes 786436
  7.2 91.1 %all-gather.8.cloned.1.call-start = ((), (), s32[]{:S(2)}) async-start(), calls=%async_computation.15 | async-start | bytes 2113536 | tf_op jit(solution)/shard_map/all_gather | solution.py:181
  7.9 149.2 %all-gather.6.cloned.1.call-start = ((), (), s32[]{:S(2)}) async-start(), calls=%async_computation.14 | async-start | bytes 2113536 | tf_op jit(solution)/shard_map/all_gather | solution.py:180
  8.7 267.1 %all-gather.10.cloned.1.call-start = ((), (), s32[]{:S(2)}) async-start(), calls=%async_computation.16 | async-start | bytes 2113536 | tf_op jit(solution)/shard_map/all_gather | solution.py:182
  9.4 306.5 %all-gather.14.cloned.1.call-start = ((), (), s32[]{:S(2)}) async-start(), calls=%async_computation.18 | async-start | bytes 8454144 | tf_op jit(solution)/shard_map/all_gather | solution.py:227
  10.0 376.5 %all-gather.12.cloned.1.call-start = ((), (), s32[]{:S(2)}) async-start(), calls=%async_computation.17 | async-start | bytes 8454144 | tf_op jit(solution)/shard_map/all_gather | solution.py:225
  14.2 88.4 %all-to-all-start = ((bf16[4,32,8]{2,0,1:T(4,128)(2,1)}), bf16[4,32,8]{2,0,1:T(4,128)(2,1)S(1)}, u32[]{:S(2)}, u32[]{:S(2)}) async-start(bf16[4,32,8]{2,0,1:T(4,128)(2,1)} %copy.112), calls=%async_computation | async-start | bytes 65536 | tf_op jit(solution)/shard_map/all_to_all | solution.py:206
  98.2 2.7 copy-start.37
  98.3 58.9 %copy-start.24 = (f32[128]{0:T(128)}, f32[128]{0:T(128)S(1)}, u32[]{:S(2)}) copy-start(f32[128]{0:T(128)S(1)} %fusion.108) | copy-start | bytes 1540
  102.6 61.7 %all-to-all-start.3 = ((bf16[4,32,8,1024]{3,2,0,1:T(8,128)(2,1)}), bf16[4,32,8,1024]{3,2,0,1:T(8,128)(2,1)S(1)}, u32[]{:S(2)}, u32[]{:S(2)}) async-start(bf16[4,32,8,1024]{3,2,0,1:T(8,128)(2,1)} %copy.126), calls=%async_computation.3 | async-start | bytes 4194304 | tf_op jit(solution)/shard_map/all_to_all | solution.py:203
  164.2 35.1 all-to-all-start.1
  170.7 47.3 %copy-start.16 = (pred[4,256,256]{1,2,0:T(8,128)(4,1)}, pred[4,256,256]{1,2,0:T(8,128)(4,1)S(1)}, u32[]{:S(2)}) copy-start(pred[4,256,256]{1,2,0:T(8,128)(4,1)S(1)} %get-tuple-element.44) | copy-start | bytes 786436
  206.0 2.6 copy-start.5
  206.5 2.1 copy-start.22
  208.6 3.5 copy-start.2
  208.6 9.3 copy-start.8
  214.1 19.8 all-to-all-start.2
  233.9 38.2 %all-to-all-start.4 = ((bf16[4,32,8,1024]{3,2,0,1:T(8,128)(2,1)}), bf16[4,32,8,1024]{3,2,0,1:T(8,128)(2,1)}, u32[]{:S(2)}, u32[]{:S(2)}) async-start(bf16[4,32,8,1024]{3,2,0,1:T(8,128)(2,1)} %copy.131), calls=%async_computation.4 | async-start | bytes 4194304 | tf_op jit(solution)/shard_map/all_to_all | solution.py:213
  241.5 813.7 %reduce-scatter.10.cloned.1.call-start = ((), (), s32[]{:S(2)}) async-start(), calls=%async_computation.21 | async-start | bytes 4227072 | tf_op jit(solution)/shard_map/reduce_scatter | solution.py:334
  275.8 40.2 %copy-start.13 = (bf16[128,1024]{1,0:T(8,128)(2,1)S(1)}, bf16[128,1024]{1,0:T(8,128)(2,1)}, u32[]{:S(2)}) copy-start(bf16[128,1024]{1,0:T(8,128)(2,1)} %param.31) | copy-start | bytes 786436
  323.5 72.0 %copy-start.32 = (f32[128]{0:T(128)S(1)}, f32[128]{0:T(128)}, u32[]{:S(2)}) copy-start(f32[128]{0:T(128)} %copy-done.31) | copy-start | bytes 1540
  323.5 72.1 %copy-start.34 = (f32[128]{0:T(128)S(1)}, f32[128]{0:T(128)}, u32[]{:S(2)}) copy-start(f32[128]{0:T(128)} %fusion.109) | copy-start | bytes 1540
  386.5 9.1 copy-start.1
  395.6 3.6 copy-start.9
  395.6 3.6 copy-start.40
  395.6 4.5 copy-start.20
  400.3 2.7 copy-start.15
  403.0 1291.8 %reduce-scatter.8.cloned.1.call-start = ((), (), s32[]{:S(2)}) async-start(), calls=%async_computation.20 | async-start | bytes 4227072 | tf_op jit(solution)/shard_map/reduce_scatter | solution.py:333
  496.1 1.6 copy-start.7
  496.1 1837.8 %reduce-scatter.6.cloned.1.call-start = ((), (), s32[]{:S(2)}) async-start(), calls=%async_computation.19 | async-start | bytes 4227072 | tf_op jit(solution)/shard_map/reduce_scatter | solution.py:332
  512.1 6.9 copy-start.6
  512.1 6.9 copy-start.19
  512.1 6.8 copy-start.21
  519.0 18.2 copy-start.23
  598.8 1.6 copy-start.11
  598.8 1.6 copy-start.14
  598.8 2397.0 %reduce-scatter.14.cloned.1.call-start = ((), (), s32[]{:S(2)}) async-start(), calls=%async_computation.23 | async-start | bytes 16908288 | tf_op jit(solution)/shard_map/reduce_scatter | solution.py:274
  608.5 1.2 copy-start.10
  608.5 1.2 copy-start.33
  608.5 1.2 copy-start.35
  608.5 3049.1 %reduce-scatter.12.cloned.1.call-start = ((), (), s32[]{:S(2)}) async-start(), calls=%async_computation.22 | async-start | bytes 16908288 | tf_op jit(solution)/shard_map/reduce_scatter | solution.py:272
  617.9 1.6 copy-start.12
  619.5 5.8 copy-start.4
  625.3 1.6 copy-start.3
  625.3 1.6 copy-start.18
  626.9 2.4 copy-start.27
  626.9 2.4 copy-start.28
  626.9 2.4 copy-start.29
  (8 other events, 6.1 us)
Sparse Core Ops, SparseCore 0:
  11.2 67.7 all-gather.7
  82.1 74.9 all-gather.5
  160.3 73.6 all-gather.9
  236.8 79.0 all-gather.13
  318.8 67.6 all-gather.11
  403.1 652.0 reduce-scatter.9
  1058.2 636.4 reduce-scatter.7
  1697.6 636.1 reduce-scatter.5
  2337.0 658.8 reduce-scatter.13
  2998.8 658.7 reduce-scatter.11
where the time goes:
time: 3670 us; the launch traced here: 3660 us
  waiting for transfers between devices  3160 us (86%)
  blocking collectives  244 us (7%)
  matrix products  130 us (4%)
  local copies, waits for them, and re-layouts  67.3 us (2%)
    reduce_scatter x1, waiting for transfers between devices, local(): lax.psum_scatter(grad_outer, ('dp', 'seq'), scatter_dimension=0, tiled=True)  662 us
    reduce_scatter x1, waiting for transfers between devices, local(): lax.psum_scatter(grad_inner, ('dp', 'seq'), scatter_dimension=0, tiled=True)  662 us
    reduce_scatter x1, waiting for transfers between devices, local(): lax.psum_scatter(grad_value, ('dp', 'seq'), scatter_dimension=0, tiled=True)  640 us
    reduce_scatter x1, waiting for transfers between devices, local(): lax.psum_scatter(grad_joint, ('dp', 'seq'), scatter_dimension=0, tiled=True)  639 us
    reduce_scatter x1, waiting for transfers between devices, local(): lax.psum_scatter(grad_output, ('dp', 'seq'), scatter_dimension=0, tiled=T...  357 us
    unnamed x2, blocking collectives  134 us
  transfers between devices with their start and end apart: 15, of which 10 were waited for; matrix products, arithmetic and copies ran while one was open for 5% of the time, Pallas kernels for 0%

commit v1 on v0

v1 whole, which is shorter than its diff:
```python
import jax
import jax.numpy as jnp
from jax import lax
from jax.experimental import pallas as pl
from jax.experimental.pallas import tpu as pltpu
from jax.sharding import Mesh, PartitionSpec as P

HEADS = 8
HEAD_DIM = 128
ROUNDS = 4
BUCKETS = 32
MOST = 8
TOK = 128
D = 1024
FF = 4096

EPS_NORM = 1e-05
EPS_KEY = 1e-06
SELF_SCORE = -10000.0
MASKED_SCORE = -1000000000.0

BF = jnp.bfloat16
F32 = jnp.float32

AXES = ("y", "z", "x", "c")
CHIPS = ("y", "z", "x")


def send(piece, axis, k):
    return lax.ppermute(piece, axis, [(i, (i + k) % 4) for i in range(4)])


def swap(piece):
    return lax.ppermute(piece, "c", [(0, 1), (1, 0)])


def gather(piece, axis):
    back, front, far = send(piece, axis, 3), send(piece, axis, 1), send(piece, axis, 2)
    return [piece, back, far, front]


def scatter(pieces, axis):
    front, back, far = (
        send(pieces[1], axis, 1),
        send(pieces[3], axis, 3),
        send(pieces[2], axis, 2),
    )
    return [pieces[0], back, far, front]


def in_order(pieces, mine):
    return jnp.roll(jnp.stack(pieces), mine, axis=0)


def reduce_over(array, axis, dim):
    mine = lax.axis_index(axis)
    parts = [
        lax.dynamic_index_in_dim(array, (mine + k) % 4, dim, keepdims=False) for k in range(4)
    ]
    got = scatter(parts, axis)
    total = got[0].astype(F32)
    for extra in got[1:]:
        total = total + extra.astype(F32)
    return total


def reduce_chips(array, order):
    left = list(CHIPS)
    for step, axis in enumerate(order):
        array = reduce_over(array, axis, left.index(axis))
        left.remove(axis)
        if step < 2:
            array = array.astype(BF)
    return array


def dot(a, b):
    return jnp.dot(a, b, preferred_element_type=F32)


def dot_t(a, b):
    return lax.dot_general(a, b, (((1,), (1,)), ((), ())), preferred_element_type=F32)


def t_dot(a, b):
    return lax.dot_general(a, b, (((0,), (0,)), ((), ())), preferred_element_type=F32)


def cost(us):
    return pl.CostEstimate(flops=int(us * 1e9), bytes_accessed=0, transcendentals=0)


def params(mib):
    return pltpu.CompilerParams(vmem_limit_bytes=mib * 1024 * 1024)


SMEM = pl.BlockSpec(memory_space=pltpu.SMEM)
VMEM = pl.BlockSpec(memory_space=pltpu.VMEM)


def iota(shape, dim):
    return lax.broadcasted_iota(jnp.int32, shape, dim)


def whole_call(kernel, name, outs, us, mib=16):
    def call(where, *arrays):
        return pl.pallas_call(
            kernel,
            in_specs=[SMEM] + [VMEM] * len(arrays),
            out_specs=[VMEM] * len(outs),
            out_shape=[jax.ShapeDtypeStruct(s, t) for s, t in outs],
            compiler_params=params(mib),
            cost_estimate=cost(us),
            name=name,
        )(where, *arrays)

    return call


def fixed(shape):
    return pl.BlockSpec(shape, lambda r: (0,) * len(shape))


def per_round(shape):
    return pl.BlockSpec((1,) + shape, lambda r: (r,) + (0,) * len(shape))


PAIRS = BUCKETS // 2


def pack_kernel(where, slab_ref, vec_ref, bucket_ref, keep_a, give_a, keep_b, give_b):
    low_core = where[3] == 0
    slab = slab_ref[...].astype(F32)
    heads = []
    for core in range(2):
        rows = []
        for h in range(4):
            cols = slice((core * 4 + h) * 128, (core * 4 + h + 1) * 128)
            rows += [slab[0:8, cols], slab[8:16, cols]]
        heads.append(jnp.concatenate(rows, axis=0))

    row, lane = iota((8, 128), 0), iota((8, 128), 1)
    vec = jnp.broadcast_to(vec_ref[0:1, :], (8, 128))
    par = jnp.zeros((8, 128), F32)
    for v in range(5):
        col = jnp.sum(jnp.where(lane == 8 * v + row, vec, 0.0), axis=1, keepdims=True)
        par = jnp.where(lane == v, col, par)
    for v in range(4):
        col = jnp.sum(jnp.where(lane == 40 + 4 * row + v, vec, 0.0), axis=1, keepdims=True)
        par = jnp.where(lane == 5 + v, col, par)

    sub, along = iota((128, 128), 0), iota((128, 128), 1)
    targets, counts = [], []
    for r in range(ROUNDS):
        chosen = jnp.broadcast_to(bucket_ref[r : r + 1, :].astype(F32), (128, 128))
        column = jnp.sum(jnp.where(sub == along, chosen, 0.0), axis=1, keepdims=True)
        earlier = (column == chosen) & (sub < along)
        rank = jnp.sum(earlier.astype(F32), axis=0, keepdims=True)
        targets.append(chosen[0:1] * MOST + rank)
        counts.append(jnp.sum((column == along.astype(F32)).astype(F32), axis=0, keepdims=True))
    aux = jnp.concatenate([par] + targets + counts, axis=0)
    keep_a[...] = jnp.concatenate([jnp.where(low_core, *heads), aux], axis=0).astype(BF)
    give_a[...] = jnp.concatenate([jnp.where(low_core, *heads[::-1]), aux], axis=0).astype(BF)

    chunks = []
    for i in range(4):
        for u in range(4):
            chunks.append(slab[24 + 8 * i : 32 + 8 * i, u * 256 : (u + 1) * 256])
    src, dst = iota((256, 256), 0), iota((256, 256), 1)
    wanted = 64 * ((dst % 128) // 32) + 32 * (dst // 128) + dst % 32
    picked = dot(jnp.concatenate(chunks, axis=0).astype(BF), (src == wanted).astype(F32).astype(BF))
    inner = []
    for core in range(2):
        halves = [
            jnp.concatenate(
                [
                    picked[t * 8 : (t + 1) * 8, core * 128 : (core + 1) * 128]
                    for t in range(half * 8, half * 8 + 8)
                ],
                axis=1,
            )
            for half in range(2)
        ]
        inner.append(jnp.concatenate(halves, axis=0))
    rest = jnp.concatenate([slab[16:24], jnp.zeros((8, D), F32)], axis=0)
    keep_b[...] = jnp.concatenate([jnp.where(low_core, *inner), rest], axis=0).astype(BF)
    give_b[...] = jnp.concatenate([jnp.where(low_core, *inner[::-1]), rest], axis=0).astype(BF)


pack = whole_call(
    pack_kernel, "pack", [((80, 128), BF)] * 2 + [((32, D), BF)] * 2, 3
)


def messages_kernel(where, keep_ref, got_ref, *outs):
    low_core = where[3] == 0
    keep, got = keep_ref[...].astype(F32), got_ref[...].astype(F32)
    first, second = jnp.where(low_core, keep, got), jnp.where(low_core, got, keep)
    aux = jnp.concatenate([first[64:72], second[64:72], first[72:80], second[72:80]], axis=0)
    heads = [
        jnp.concatenate(
            [
                first[h * 16 : h * 16 + 8], second[h * 16 : h * 16 + 8],
                first[h * 16 + 8 : h * 16 + 16], second[h * 16 + 8 : h * 16 + 16],
            ],
            axis=0,
        )
        for h in range(4)
    ]
    for k in range(4):
        head = (where[1] + k) % 4
        rows = heads[0]
        for h in range(1, 4):
            rows = jnp.where(head == h, heads[h], rows)
        outs[k][...] = jnp.concatenate([rows, aux], axis=0).astype(BF)


messages = whole_call(messages_kernel, "messages", [((64, 128), BF)] * 4, 1)


def payload_kernel(where, keep_ref, got_ref, outer_ref, out_ref):
    low_core = where[3] == 0
    keep, got = keep_ref[...].astype(F32), got_ref[...].astype(F32)
    first, second = jnp.where(low_core, keep, got), jnp.where(low_core, got, keep)
    for at, to in ((0, 0), (8, 16), (16, 64)):
        out_ref[to : to + 16, :] = jnp.concatenate(
            [first[at : at + 8], second[at : at + 8]], axis=0
        ).astype(BF)
    out_ref[32:64, :] = outer_ref[...]


payload = whole_call(payload_kernel, "payload", [((80, D), BF)], 1)


def assemble_kernel(where, x0, x1, x2, x3, w_ref, par_ref, tgt_ref, tgt_t_ref, count_ref, par_rows):
    for m, piece in enumerate((x0, x1, x2, x3)):
        for n in range(4):
            for k in range(4):
                chip = ((where[0] + n) % 4 * 4 + (where[1] + k) % 4) * 4 + (where[2] + m) % 4
                to = pl.ds(pl.multiple_of(chip * 16, 16), 16)
                at = (n * 4 + k) * 48
                w_ref[to, :128] = piece[at : at + 16, :]
                w_ref[to, 128:] = piece[at + 16 : at + 32, :]
                par_rows[to, :] = piece[at + 32 : at + 48, :]
    par_t = jnp.transpose(par_rows[...].astype(F32))
    par_ref[...] = par_t[:16, :]
    empty = jnp.zeros((96, 128), F32)
    slots = [piece[768:832, :].astype(F32) for piece in (x0, x1, x2, x3)]
    for r in range(ROUNDS):
        rows = jnp.concatenate(
            [slots[m][s * 8 + r : s * 8 + r + 1] for m in range(4) for s in range(8)], axis=0
        )
        tgt_ref[r] = rows.astype(jnp.int32)
        tgt_t_ref[r] = jnp.transpose(jnp.concatenate([rows, empty], axis=0)).astype(jnp.int32)
        count_ref[r] = jnp.concatenate(
            [slots[m][s * 8 + 4 + r : s * 8 + 5 + r] for m in range(4) for s in range(8)], axis=0
        )


def assemble(where, *pieces):
    shapes = [
        ((D, 256), BF), ((16, D), F32), ((ROUNDS, 32, 128), jnp.int32),
        ((ROUNDS, 128, 128), jnp.int32), ((ROUNDS, 32, 128), F32),
    ]
    return pl.pallas_call(
        assemble_kernel,
        in_specs=[SMEM] + [VMEM] * 4,
        out_specs=[VMEM] * 5,
        out_shape=[jax.ShapeDtypeStruct(s, t) for s, t in shapes],
        scratch_shapes=[pltpu.VMEM((D, 128), BF)],
        compiler_params=params(16),
        cost_estimate=cost(2),
        name="assemble",
    )(where, *pieces)


def mask_kernel(where, count_ref, mask_ref):
    z, x, c = where[1], where[2], where[3]
    shape = (256, 128)
    row, lane = iota(shape, 0), iota(shape, 1)
    source, rank = row >> 3, row & 7
    of_chip = lambda z_of, x_of, core: ((z_of & 3) * 8 + (x_of & 3) * 2 + core) * 8
    kpos = of_chip(z + ((source >> 1) & 3), x + (source >> 3), source & 1) + rank
    asker = (lane >> 3) & 7
    qpos = of_chip(z + (asker >> 1), x, asker & 1) + (lane & 7)
    code = jnp.where(kpos == qpos, -1.0, jnp.where(kpos < qpos, 0.0, -1e5))
    rank_f = rank.astype(F32)
    expand = (iota((256, 32), 0) >> 3) == iota((256, 32), 1)
    by_slot = dot(expand.astype(F32).astype(BF), count_ref[0].astype(BF)).astype(BF)
    bucket, side = iota((128, 128), 0), iota((128, 128), 1) >> 6

    @pl.loop(0, PAIRS, unroll=4)
    def _(p):
        select = (bucket == 2 * p + side).astype(F32).astype(BF)
        live = rank_f < dot(by_slot, select)
        mask_ref[0, p] = jnp.where(live, code, -1e5).astype(BF)


def make_mask(where, counts):
    return pl.pallas_call(
        mask_kernel,
        grid=(ROUNDS,),
        in_specs=[SMEM, per_round((32, 128))],
        out_specs=per_round((PAIRS, 256, 128)),
        out_shape=jax.ShapeDtypeStruct((ROUNDS, PAIRS, 256, 128), BF),
        compiler_params=params(16),
        cost_estimate=cost(6),
        name="make_mask",
    )(where, counts)


def token_rows(where, own0, own3, sib0, sib3):
    step = pl.program_id(0)
    own = step % 2 == where[3]
    near = jnp.where(own, own0[...].astype(F32), sib0[0].astype(F32))
    far = jnp.where(own, own3[0].astype(F32), sib3[0].astype(F32))
    return jnp.where(step < 2, near, far), own


def token_specs():
    far = pl.BlockSpec((1, TOK, D), lambda i: (jnp.maximum(i // 2 - 1, 0), 0, 0))
    return [
        pl.BlockSpec((TOK, D), lambda i: (0, 0)),
        far,
        pl.BlockSpec((1, TOK, D), lambda i: (0, 0, 0)),
        far,
    ]


def project_kernel(where, own0, own3, sib0, sib3, par_ref, w_ref, normed_ref, qv_ref):
    rows, _ = token_rows(where, own0, own3, sib0, sib3)
    centered = rows - jnp.mean(rows, axis=-1, keepdims=True)
    spread = jnp.mean(centered * centered, axis=-1, keepdims=True)
    normed = centered * lax.rsqrt(spread + EPS_NORM) * par_ref[0:1, :] + par_ref[1:2, :]
    normed = normed.astype(BF)
    normed_ref[...] = normed
    qv_ref[...] = dot(normed, w_ref[...]).astype(BF)


def project(where, tokens, par, w):
    whole = lambda i: (0, 0)
    return pl.pallas_call(
        project_kernel,
        grid=(8,),
        in_specs=[SMEM] + token_specs()
        + [pl.BlockSpec((16, D), whole), pl.BlockSpec((D, 256), whole)],
        out_specs=[
            pl.BlockSpec((TOK, D), lambda i: (i, 0)),
            pl.BlockSpec((TOK, 256), lambda i: (i, 0)),
        ],
        out_shape=[
            jax.ShapeDtypeStruct((8 * TOK, D), BF),
            jax.ShapeDtypeStruct((8 * TOK, 256), BF),
        ],
        compiler_params=params(24),
        cost_estimate=cost(4),
        name="project",
    )(where, *tokens, par, w)


def project_back_kernel(
    where, own0, own3, sib0, sib3, par_ref, w_ref, normed_ref, qv_ref, gq_ref, g0, g1, g2, g3,
    own_out, sib_out, wg_ref, total, sums,
):
    step = pl.program_id(0)
    x, own = token_rows(where, own0, own3, sib0, sib3)
    q = qv_ref[:, :HEAD_DIM].astype(F32)
    inv = lax.rsqrt(jnp.sum(q * q, axis=-1, keepdims=True) + EPS_KEY)
    grad = g0[...].astype(F32) + g1[...].astype(F32) + g2[...].astype(F32) + g3[...].astype(F32)
    gk = grad[:, :HEAD_DIM]
    along = jnp.sum(q * gk, axis=-1, keepdims=True)
    gq = gq_ref[...] + gk * inv - q * (inv * inv * inv * along)
    rows = jnp.concatenate([gq.astype(BF), grad[:, HEAD_DIM:].astype(BF)], axis=1)
    back = dot_t(rows, w_ref[...])

    @pl.when(own)
    def _():
        own_out[0] = back.astype(BF)

    @pl.when(jnp.logical_not(own))
    def _():
        sib_out[0] = back.astype(BF)

    centered = x - jnp.mean(x, axis=-1, keepdims=True)
    spread = jnp.mean(centered * centered, axis=-1, keepdims=True)
    xhat = centered * lax.rsqrt(spread + EPS_NORM)
    gain_part = jnp.sum((back * xhat).reshape(TOK // 8, 8, D), axis=0)
    shift_part = jnp.sum(back.reshape(TOK // 8, 8, D), axis=0)
    weight_part = t_dot(normed_ref[...], rows)

    @pl.when(step == 0)
    def _():
        total[...] = weight_part
        sums[0:8, :] = gain_part
        sums[8:16, :] = shift_part

    @pl.when(step > 0)
    def _():
        total[...] += weight_part
        sums[0:8, :] += gain_part
        sums[8:16, :] += shift_part

    @pl.when(step == 7)
    def _():
        wg_ref[:, :256] = total[...].astype(BF)
        gain_sum = jnp.sum(sums[0:8, :], axis=0, keepdims=True)
        shift_sum = jnp.sum(sums[8:16, :], axis=0, keepdims=True)
        both = jnp.where(iota((HEAD_DIM, D), 0) < 64, gain_sum, shift_sum)
        wg_ref[:, 256:] = jnp.transpose(both).astype(BF)


def project_back(where, tokens, par, w, normed, qv, gq, pieces):
    token_block = pl.BlockSpec((1, TOK, D), lambda i: (i // 2, 0, 0))
    whole = lambda i: (0, 0)
    row_block = lambda width: pl.BlockSpec((TOK, width), lambda i: (i, 0))
    return pl.pallas_call(
        project_back_kernel,
        grid=(8,),
        in_specs=[SMEM] + token_specs()
        + [
            pl.BlockSpec((16, D), whole),
            pl.BlockSpec((D, 256), whole),
            row_block(D),
            row_block(256),
            row_block(HEAD_DIM),
        ]
        + [row_block(256)] * 4,
        out_specs=[token_block, token_block, pl.BlockSpec((D, 384), whole)],
        out_shape=[
            jax.ShapeDtypeStruct((4, TOK, D), BF),
            jax.ShapeDtypeStruct((4, TOK, D), BF),
            jax.ShapeDtypeStruct((D, 384), BF),
        ],
        scratch_shapes=[pltpu.VMEM((D, 256), F32), pltpu.VMEM((16, D), F32)],
        compiler_params=params(32),
        cost_estimate=cost(8),
        name="project_back",
    )(where, *tokens, par, w, normed, qv, gq, *pieces)


def chip_rows(where, own, sib):
    low_core = where[3] == 0
    return jnp.concatenate([jnp.where(low_core, own, sib), jnp.where(low_core, sib, own)], axis=0)


def normalized(values):
    centered = values - jnp.mean(values, axis=-1, keepdims=True)
    spread = jnp.mean(centered * centered, axis=-1, keepdims=True)
    scale = lax.rsqrt(spread + EPS_NORM)
    return centered * scale, scale


def norm_back(u, xhat, scale):
    mean_u = jnp.mean(u, axis=-1, keepdims=True)
    mean_ux = jnp.mean(u * xhat, axis=-1, keepdims=True)
    return (u - mean_u - xhat * mean_ux) * scale


def head_rows(w_ref, head):
    return w_ref[pl.ds(head * 8, 8)].reshape(HEAD_DIM, D)


def heads_of(where):
    for side in range(2):
        core = where[3] if side == 0 else 1 - where[3]
        for m in range(4):
            yield side, m, core * 4 + (where[1] + m) % 4


GELU_IN = 0.7978845608028654
GELU_CUBE = 0.044715


def feed_kernel(
    where, mix_own, mix_sib, first_own, first_sib, cot_own, cot_sib, par_ref, bias_ref,
    out_w, inner_ref, outer_ref,
    sum_ref, first_out, input_t_ref, active_ref, grad_ref, back_ref, hid_sum_ref,
    ffn_in, cot_t, back_t,
):
    step = pl.program_id(0)

    @pl.when(step == 0)
    def _():
        total = chip_rows(where, first_own[...].astype(F32), first_sib[0].astype(F32))
        mixes = (mix_own, mix_sib)
        for side, m, head in heads_of(where):
            total = total + dot(mixes[side][:, m * 128 : m * 128 + 128], head_rows(out_w, head))
        sum_ref[...] = total
        own = jnp.where(where[3] == 0, total[:TOK], total[TOK:])
        first_out[...] = own.astype(BF)
        xhat, _ = normalized(total)
        rows = xhat * par_ref[2:3, :] + par_ref[3:4, :]
        ffn_in[...] = rows.astype(BF)
        input_t_ref[...] = jnp.transpose(rows).astype(BF)
        cot = chip_rows(where, cot_own[...].astype(F32), cot_sib[0].astype(F32))
        cot_t[...] = jnp.transpose(cot).astype(BF)

    inner = inner_ref[...].reshape(D, 256)
    outer = outer_ref[...].reshape(256, D)
    hidden = dot(ffn_in[...], inner) + bias_ref[0:1, :]
    square = hidden * hidden
    bent = jnp.tanh(GELU_IN * hidden * (1.0 + GELU_CUBE * square))
    half = 0.5 * (1.0 + bent)
    active_ref[...] = (hidden * half).astype(BF)
    slope = half + 0.5 * hidden * (1.0 - bent * bent) * GELU_IN * (
        1.0 + 3.0 * GELU_CUBE * square
    )
    grad_active = jnp.transpose(dot(outer, cot_t[...]))
    grad = (grad_active * slope).astype(BF)
    grad_ref[...] = grad
    hid_sum_ref[...] = jnp.broadcast_to(
        jnp.sum(grad.astype(F32), axis=0, keepdims=True), (8, 256)
    )
    part = dot(inner, jnp.transpose(grad))

    @pl.when(step == 0)
    def _():
        back_t[...] = part

    @pl.when(step > 0)
    def _():
        back_t[...] += part

    @pl.when(step == 7)
    def _():
        back_ref[...] = jnp.transpose(back_t[...])


def feed(where, mix_own, mix_sib, first_in, cot_second, sib_rows, par, bias, gathered):
    whole = lambda i: (0, 0)
    two = 2 * TOK
    return pl.pallas_call(
        feed_kernel,
        grid=(8,),
        in_specs=[
            SMEM,
            pl.BlockSpec((two, 512), whole),
            pl.BlockSpec((two, 512), whole),
            pl.BlockSpec((TOK, D), whole),
            pl.BlockSpec((1, TOK, D), lambda i: (1, 0, 0)),
            pl.BlockSpec((TOK, D), whole),
            pl.BlockSpec((1, TOK, D), lambda i: (3, 0, 0)),
            pl.BlockSpec((16, D), whole),
            pl.BlockSpec((8, 256), lambda i: (0, i)),
            pl.BlockSpec((64, 16, D), lambda i: (0, 4, 0)),
            pl.BlockSpec((64, 16, 256), lambda i: (0, i // 4, i % 4)),
            pl.BlockSpec((8, 32, D), lambda i: (i, 1, 0)),
        ],
        out_specs=[
            pl.BlockSpec((two, D), whole),
            pl.BlockSpec((TOK, D), whole),
            pl.BlockSpec((D, two), whole),
            pl.BlockSpec((two, 256), lambda i: (0, i)),
            pl.BlockSpec((two, 256), lambda i: (0, i)),
            pl.BlockSpec((two, D), whole),
            pl.BlockSpec((8, 256), lambda i: (0, i)),
        ],
        out_shape=[
            jax.ShapeDtypeStruct((two, D), F32),
            jax.ShapeDtypeStruct((TOK, D), BF),
            jax.ShapeDtypeStruct((D, two), BF),
            jax.ShapeDtypeStruct((two, 2048), BF),
            jax.ShapeDtypeStruct((two, 2048), BF),
            jax.ShapeDtypeStruct((two, D), F32),
            jax.ShapeDtypeStruct((8, 2048), F32),
        ],
        scratch_shapes=[
            pltpu.VMEM((two, D), BF),
            pltpu.VMEM((D, two), BF),
            pltpu.VMEM((D, two), F32),
        ],
        compiler_params=params(40),
        cost_estimate=cost(16),
        name="feed",
    )(
        where, mix_own, mix_sib, first_in, sib_rows, cot_second, sib_rows, par, bias,
        gathered, gathered, gathered,
    )


def first_back_kernel(
    where, back_own, back_sib, sum_ref, cot_own, cot_sib, par_ref, out_w,
    grad_first, branch_ref, m0, m1, m2, m3, sums_ref,
):
    back = back_own[...] + back_sib[...]
    xhat, scale = normalized(sum_ref[...])
    total = chip_rows(where, cot_own[...].astype(F32), cot_sib[0].astype(F32))
    total = total + norm_back(back * par_ref[2:3, :], xhat, scale)
    branch = total.astype(BF)
    branch_ref[...] = branch
    grad_first[...] = jnp.where(where[3] == 0, total[:TOK], total[TOK:]).astype(BF)
    outs = (m0, m1, m2, m3)
    for side, m, head in heads_of(where):
        if side == 0:
            outs[m][...] = dot_t(branch, head_rows(out_w, head)).astype(BF)
    gain = jnp.sum(back * xhat, axis=0, keepdims=True)
    shift = jnp.sum(back, axis=0, keepdims=True)
    sums_ref[...] = jnp.concatenate([gain, shift, jnp.zeros((6, D), F32)], axis=0)


def first_back(where, back_own, back_sib, first_sum, cot_first, sib_rows, par, gathered):
    two = 2 * TOK
    one = lambda shape: pl.BlockSpec(shape, lambda i: (0,) * len(shape))
    return pl.pallas_call(
        first_back_kernel,
        grid=(1,),
        in_specs=[
            SMEM, one((two, D)), one((two, D)), one((two, D)), one((TOK, D)),
            pl.BlockSpec((1, TOK, D), lambda i: (2, 0, 0)),
            one((16, D)),
            pl.BlockSpec((64, 16, D), lambda i: (0, 4, 0)),
        ],
        out_specs=[one((TOK, D)), one((two, D))] + [one((two, 128))] * 4 + [one((8, D))],
        out_shape=[jax.ShapeDtypeStruct((TOK, D), BF), jax.ShapeDtypeStruct((two, D), BF)]
        + [jax.ShapeDtypeStruct((two, 128), BF)] * 4
        + [jax.ShapeDtypeStruct((8, D), F32)],
        compiler_params=params(40),
        cost_estimate=cost(6),
        name="first_back",
    )(where, back_own, back_sib, first_sum, cot_first, sib_rows, par, gathered)


def weights_kernel(
    where, active_ref, grad_ref, input_t, cot_own, cot_sib, mix_own, mix_sib, branch_ref, outer_ref,
    gi_ref, go_ref, gw_ref, own_ref, give_ref, cot_sum_ref, cot, total,
):
    step = pl.program_id(0)

    @pl.when(step == 0)
    def _():
        rows = chip_rows(where, cot_own[...].astype(F32), cot_sib[0].astype(F32))
        cot[...] = rows.astype(BF)
        cot_sum_ref[...] = jnp.broadcast_to(jnp.sum(rows, axis=0, keepdims=True), (8, D))
        total[...] = jnp.zeros_like(total)
        low_core = where[3] == 0
        cols = jnp.where(
            low_core, branch_ref[:, :512].astype(F32), branch_ref[:, 512:].astype(F32)
        ).astype(BF)
        mixes = (mix_own, mix_sib)
        for side, m, head in heads_of(where):
            rows = t_dot(mixes[side][:, m * 128 : m * 128 + 128], cols)
            gw_ref[pl.ds(head * 8, 8)] = rows.astype(BF).reshape(8, 16, 512)

    active = active_ref[...]
    total[...] += dot(active, outer_ref[...].reshape(256, D))
    gi_ref[...] = dot(input_t[...], grad_ref[...]).astype(BF).reshape(64, 16, 256)
    go_ref[...] = t_dot(active, cot[...]).astype(BF).reshape(8, 32, D)

    @pl.when(step == 7)
    def _():
        low_core = where[3] == 0
        own_ref[...] = jnp.where(low_core, total[:TOK], total[TOK:])
        give_ref[...] = jnp.where(low_core, total[TOK:], total[:TOK])


def weight_grads(
    where, active, grad, input_t, cot_second, sib_rows, mix_own, mix_sib, branch, gathered
):
    two = 2 * TOK
    whole = lambda i: (0, 0)
    return pl.pallas_call(
        weights_kernel,
        grid=(8,),
        in_specs=[
            SMEM,
            pl.BlockSpec((two, 256), lambda i: (0, i)),
            pl.BlockSpec((two, 256), lambda i: (0, i)),
            pl.BlockSpec((D, two), whole),
            pl.BlockSpec((TOK, D), whole),
            pl.BlockSpec((1, TOK, D), lambda i: (3, 0, 0)),
            pl.BlockSpec((two, 512), whole),
            pl.BlockSpec((two, 512), whole),
            pl.BlockSpec((two, D), whole),
            pl.BlockSpec((8, 32, D), lambda i: (i, 1, 0)),
        ],
        out_specs=[
            pl.BlockSpec((64, 16, 256), lambda i: (0, 0, i)),
            pl.BlockSpec((8, 32, D), lambda i: (i, 0, 0)),
            pl.BlockSpec((64, 16, 512), lambda i: (0, 0, 0)),
            pl.BlockSpec((TOK, D), whole),
            pl.BlockSpec((TOK, D), whole),
            pl.BlockSpec((8, D), whole),
        ],
        out_shape=[
            jax.ShapeDtypeStruct((64, 16, 2048), BF),
            jax.ShapeDtypeStruct((64, 32, D), BF),
            jax.ShapeDtypeStruct((64, 16, 512), BF),
            jax.ShapeDtypeStruct((TOK, D), F32),
            jax.ShapeDtypeStruct((TOK, D), F32),
            jax.ShapeDtypeStruct((8, D), F32),
        ],
        scratch_shapes=[pltpu.VMEM((two, D), BF), pltpu.VMEM((two, D), F32)],
        compiler_params=params(40),
        cost_estimate=cost(14),
        name="weight_grads",
    )(where, active, grad, input_t, cot_second, sib_rows, mix_own, mix_sib, branch, gathered)


def make_keys(pieces, kv_rows):
    for m, piece in enumerate(pieces):

        @pl.loop(0, 8)
        def _(s, m=m, piece=piece):
            rows = pl.ds(pl.multiple_of(s * TOK, TOK), TOK)
            to = pl.ds(pl.multiple_of(m * 8 * TOK + s * TOK, TOK), TOK)
            q = piece[rows, :HEAD_DIM].astype(F32)
            inv = lax.rsqrt(jnp.sum(q * q, axis=-1, keepdims=True) + EPS_KEY)
            kv_rows[to, :HEAD_DIM] = (q * inv).astype(BF)
            kv_rows[to, HEAD_DIM:] = piece[rows, HEAD_DIM:]


def round_weights(lt_ref, at):
    totals = [lt_ref[r, at, :].astype(F32) for r in range(ROUNDS)]
    peak = jnp.maximum(jnp.maximum(totals[0], totals[1]), jnp.maximum(totals[2], totals[3]))
    exps = [jnp.exp(t - peak) for t in totals]
    scale = 1.0 / (exps[0] + exps[1] + exps[2] + exps[3])
    return [e * scale for e in exps]


def hot_slots(tgt_ref, source):
    slots = lax.broadcasted_iota(jnp.int32, (BUCKETS * MOST, TOK), 0)
    return (slots == tgt_ref[0, pl.ds(source, 1), :]).astype(F32).astype(BF)


def hot_tokens(tgt_t_ref, source):
    slots = lax.broadcasted_iota(jnp.int32, (TOK, BUCKETS * MOST), 1)
    return (slots == tgt_t_ref[0, :, source : source + 1]).astype(F32).astype(BF)


def spread(first, second):
    width = first.shape[-1]
    both = [a.reshape(PAIRS, 2, MOST, width) for a in (first, second)]
    return jnp.concatenate(both, axis=2).astype(BF)


def two_sources(pair):
    return pl.ds(pl.multiple_of(pair * 16, 16), 16)


def fill_keys(pieces, tgt_ref, kv_rows, kv_ref):
    @pl.loop(0, 16, unroll=4)
    def _(pair):
        placed = []
        for half in range(2):
            source = pair * 2 + half
            rows = kv_rows[pl.ds(pl.multiple_of(source * TOK, TOK), TOK), :]
            placed.append(dot(hot_slots(tgt_ref, source), rows))
        both = spread(*placed)
        at = two_sources(pair)
        for low in range(2):
            kv_ref[0, :, at, low * 128 : low * 128 + 128] = both[:, low, :, :128]
            kv_ref[0, :, at, 256 + low * 128 : 384 + low * 128] = both[:, low, :, 128:]


def place_diagonal(both, ref, pair):
    at = pl.multiple_of(pair * 16, 16)
    empty = jnp.zeros((PAIRS, 16, 128), BF)
    ref[:, pl.ds(at, 16), :128] = both[:, 0]
    ref[:, pl.ds(at, 16), 128:] = empty
    ref[:, pl.ds(64 + at, 16), :128] = empty
    ref[:, pl.ds(64 + at, 16), 128:] = both[:, 1]


def eye():
    return lax.broadcasted_iota(jnp.int32, (128, 128), 0) == lax.broadcasted_iota(
        jnp.int32, (128, 128), 1
    )


def pair_softmax(keys, queries, code):
    scores = dot_t(keys, queries)
    scores = jnp.where(code == 0.0, scores, code * 1e4)
    peak = jnp.max(scores, axis=0, keepdims=True)
    exponent = jnp.exp(scores - peak)
    total = jnp.sum(exponent, axis=0, keepdims=True)
    return exponent * (1.0 / total), peak + jnp.log(total)


def attend_kernel(
    p0, p1, p2, p3, tgt_ref, tgt_t_ref, mask_ref,
    mixed_ref, ro_ref, lt_ref, kv_ref, qm_ref, kv_rows, att,
):
    this_round = pl.program_id(0)
    pieces = (p0, p1, p2, p3)

    @pl.when(this_round == 0)
    def _():
        make_keys(pieces, kv_rows)

    fill_keys(pieces, tgt_ref, kv_rows, kv_ref)

    @pl.loop(0, 4, unroll=4)
    def _(pair):
        placed = []
        for half in range(2):
            source = pair * 2 + half
            rows = p0[pl.ds(pl.multiple_of(source * TOK, TOK), TOK), :HEAD_DIM]
            placed.append(dot(hot_slots(tgt_ref, source), rows))
        place_diagonal(spread(*placed), qm_ref.at[0], pair)

    ones = jnp.ones((128, 128), BF)

    @pl.loop(0, PAIRS, unroll=16)
    def _(p):
        code = mask_ref[0, p].astype(F32)
        probs, log_total = pair_softmax(kv_ref[0, p, :, :256], qm_ref[0, p], code)
        out = t_dot(probs.astype(BF), kv_ref[0, p, :, 256:])
        logs = dot(jnp.where(eye(), log_total, 0.0).astype(BF), ones)
        att[p, 0, :, :128] = out[:64, :128]
        att[p, 1, :, :128] = out[64:, 128:]
        att[p, 0, :, 128:] = logs[:64]
        att[p, 1, :, 128:] = logs[64:]

    for s in range(8):
        slots = att[:, :, s * MOST : (s + 1) * MOST, :].reshape(256, 256)
        rows = dot(hot_tokens(tgt_t_ref, s), slots.astype(BF)).astype(BF)
        ro_ref[this_round, s * TOK : (s + 1) * TOK, :] = rows[:, :HEAD_DIM]
        lt_ref[this_round, s * TOK : (s + 1) * TOK, :] = rows[:, HEAD_DIM:]

    @pl.when(this_round == ROUNDS - 1)
    def _():
        @pl.loop(0, 8)
        def _(s):
            at = pl.ds(pl.multiple_of(s * TOK, TOK), TOK)
            weights = round_weights(lt_ref, at)
            mixed = weights[0] * ro_ref[0, at, :].astype(F32)
            for r in range(1, ROUNDS):
                mixed = mixed + weights[r] * ro_ref[r, at, :].astype(F32)
            mixed_ref[at, :] = mixed.astype(BF)


def attend(pieces, tgt, tgt_t, mask):
    rows = 8 * TOK
    return pl.pallas_call(
        attend_kernel,
        grid=(ROUNDS,),
        in_specs=[fixed((rows, 256))] * 4
        + [per_round((32, TOK)), per_round((TOK, 128)), per_round((PAIRS, 256, 128))],
        out_specs=[
            fixed((rows, HEAD_DIM)),
            fixed((ROUNDS, rows, HEAD_DIM)),
            fixed((ROUNDS, rows, HEAD_DIM)),
            per_round((PAIRS, 256, 512)),
            per_round((PAIRS, 128, 256)),
        ],
        out_shape=[
            jax.ShapeDtypeStruct((rows, HEAD_DIM), BF),
            jax.ShapeDtypeStruct((ROUNDS, rows, HEAD_DIM), BF),
            jax.ShapeDtypeStruct((ROUNDS, rows, HEAD_DIM), BF),
            jax.ShapeDtypeStruct((ROUNDS, PAIRS, 256, 512), BF),
            jax.ShapeDtypeStruct((ROUNDS, PAIRS, 128, 256), BF),
        ],
        scratch_shapes=[
            pltpu.VMEM((4 * rows, 256), BF),
            pltpu.VMEM((PAIRS, 2, 64, 256), F32),
        ],
        compiler_params=params(40),
        cost_estimate=cost(24),
        name="attend",
    )(*pieces, tgt, tgt_t, mask)


def attend_back_kernel(
    tgt_ref, tgt_t_ref, mask_ref, kv_ref, qm_ref, ro_ref, lt_ref, gm_ref,
    gq_ref, gkv_ref, gd, gt_slots, gq_slots, gkv_slots, gkv_rows,
):
    this_round = pl.program_id(0)

    @pl.when(this_round == 0)
    def _():
        gq_ref[...] = jnp.zeros_like(gq_ref)
        gkv_rows[...] = jnp.zeros_like(gkv_rows)

    @pl.loop(0, 4, unroll=4)
    def _(pair):
        placed = []
        for half in range(2):
            source = pair * 2 + half
            at = pl.ds(pl.multiple_of(source * TOK, TOK), TOK)
            weights = round_weights(lt_ref, at)
            grad = gm_ref[at, :].astype(F32)
            agree = [
                jnp.sum(grad * ro_ref[r, at, :].astype(F32), axis=-1, keepdims=True)
                for r in range(ROUNDS)
            ]
            mean = weights[0] * agree[0]
            for r in range(1, ROUNDS):
                mean = mean + weights[r] * agree[r]
            weight, mine = weights[0], agree[0]
            for r in range(1, ROUNDS):
                weight = jnp.where(this_round == r, weights[r], weight)
                mine = jnp.where(this_round == r, agree[r], mine)
            rows = jnp.concatenate(
                [(weight * grad).astype(BF), (weight * (mine - mean)).astype(BF)], axis=1
            )
            placed.append(dot(hot_slots(tgt_ref, source), rows))
        both = spread(*placed)
        place_diagonal(both[..., :128], gd, pair)
        at = pl.multiple_of(pair * 16, 16)
        gt_slots[:, pl.ds(at, 16), :] = both[:, 0, :, 128:]
        gt_slots[:, pl.ds(64 + at, 16), :] = both[:, 1, :, 128:]

    @pl.loop(0, PAIRS, unroll=16)
    def _(p):
        code = mask_ref[0, p].astype(F32)
        keys, values = kv_ref[0, p, :, :256], kv_ref[0, p, :, 256:]
        queries, grads = qm_ref[0, p], gd[p]
        probs, _ = pair_softmax(keys, queries, code)
        grad_probs = dot_t(values, grads)
        agreement = jnp.sum(probs * grad_probs, axis=0, keepdims=True)
        grad_log = jnp.sum(jnp.where(eye(), gt_slots[p].astype(F32), 0.0), axis=0, keepdims=True)
        grad_scores = probs * (grad_probs + (grad_log - agreement))
        grad_scores = jnp.where(code == 0.0, grad_scores, 0.0).astype(BF)
        grad_keys = dot(grad_scores, queries)
        grad_values = dot(probs.astype(BF), grads)
        grad_queries = t_dot(grad_scores, keys)
        gq_slots[p, 0] = grad_queries[:64, :128]
        gq_slots[p, 1] = grad_queries[64:, 128:]
        for low in range(2):
            gkv_slots[p, low, :, :128] = grad_keys[:, low * 128 : low * 128 + 128]
            gkv_slots[p, low, :, 128:] = grad_values[:, low * 128 : low * 128 + 128]

    for s in range(32):
        slots = gkv_slots[:, :, s * MOST : (s + 1) * MOST, :].reshape(256, 256)
        gkv_rows[s * TOK : (s + 1) * TOK, :] += dot(hot_tokens(tgt_t_ref, s), slots.astype(BF))
    for s in range(8):
        slots = gq_slots[:, :, s * MOST : (s + 1) * MOST, :].reshape(256, HEAD_DIM)
        gq_ref[s * TOK : (s + 1) * TOK, :] += dot(hot_tokens(tgt_t_ref, s), slots.astype(BF))

    @pl.when(this_round == ROUNDS - 1)
    def _():
        for m in range(4):
            gkv_ref[m] = gkv_rows[m * 8 * TOK : (m + 1) * 8 * TOK, :].astype(BF)


def attend_back(tgt, tgt_t, mask, kv, qm, ro, lt, gm):
    rows = 8 * TOK
    return pl.pallas_call(
        attend_back_kernel,
        grid=(ROUNDS,),
        in_specs=[
            per_round((32, TOK)),
            per_round((TOK, 128)),
            per_round((PAIRS, 256, 128)),
            per_round((PAIRS, 256, 512)),
            per_round((PAIRS, 128, 256)),
            fixed((ROUNDS, rows, HEAD_DIM)),
            fixed((ROUNDS, rows, HEAD_DIM)),
            fixed((rows, HEAD_DIM)),
        ],
        out_specs=[fixed((rows, HEAD_DIM)), fixed((4, rows, 256))],
        out_shape=[
            jax.ShapeDtypeStruct((rows, HEAD_DIM), F32),
            jax.ShapeDtypeStruct((4, rows, 256), BF),
        ],
        scratch_shapes=[
            pltpu.VMEM((PAIRS, 128, 256), BF),
            pltpu.VMEM((PAIRS, 128, 128), BF),
            pltpu.VMEM((PAIRS, 2, 64, HEAD_DIM), F32),
            pltpu.VMEM((PAIRS, 2, 256, 256), F32),
            pltpu.VMEM((4 * rows, 256), F32),
        ],
        compiler_params=params(56),
        cost_estimate=cost(38),
        name="attend_back",
    )(tgt, tgt_t, mask, kv, qm, ro, lt, gm)


def local(
    first_in, second_in, attn_gain, attn_shift, w_joint, w_value, w_output, ffn_gain, ffn_shift,
    w_inner, b_inner, w_outer, b_outer, buckets, cot_first, cot_second,
):
    y, z, x, c = (lax.axis_index(a) for a in AXES)
    where = jnp.stack([y, z, x, c]).astype(jnp.int32)
    low_core = c == 0

    def by_core(first, second):
        return jnp.where(low_core, first, second)

    sib_rows = swap(jnp.stack([second_in, first_in, cot_first, cot_second]))
    tok_far = jnp.stack(gather(second_in, "z")[1:])
    tokens = (second_in, tok_far, sib_rows, swap(tok_far))

    slab = jnp.concatenate(
        [w_joint, w_value, w_output]
        + [w_inner[:, i * D : (i + 1) * D] for i in range(4)]
        + [jnp.zeros((8, D), BF)]
    )
    vec = jnp.concatenate(
        [attn_gain, attn_shift, ffn_gain, ffn_shift, b_outer, b_inner, jnp.zeros((56,), BF)]
    ).astype(F32)
    keep_a, give_a, keep_b, give_b = pack(where, slab, vec.reshape(1, 128), buckets[:, :, 0])
    got_a, got_b = swap(give_a), swap(give_b)
    gathered = lax.all_gather(
        payload(where, keep_b, got_b, w_outer)[0], CHIPS, axis=0, tiled=False
    ).reshape(64, 80, D)
    z_got = scatter(messages(where, keep_a, got_a), "z")
    y_got = gather(jnp.concatenate([piece[:48] for piece in z_got]), "y")
    x_got = gather(jnp.concatenate(y_got + [piece[48:] for piece in z_got]), "x")
    w_qv, par, tgt, tgt_t, counts = assemble(where, *x_got)
    bias_inner = par[5:9].reshape(4, 64, 2, 8)
    bias_inner = by_core(bias_inner[:, :, 0], bias_inner[:, :, 1])
    bias_inner = jnp.transpose(bias_inner, (1, 2, 0)).reshape(1, 2048)
    bias_inner = jnp.broadcast_to(bias_inner, (8, 2048))

    normed, qv = project(where, tokens, par, w_qv)
    pieces = gather(qv, "x")
    mask = make_mask(where, counts)
    mixed_head, round_out, round_total, kv, qm = attend(pieces, tgt, tgt_t, mask)

    mix_own = jnp.concatenate(
        scatter([mixed_head[k * 256 : (k + 1) * 256] for k in range(4)], "z"), axis=1
    )
    mix_sib = swap(mix_own)
    first_sum, first_out, input_t, active, grad_hidden, back, hid_sum = feed(
        where, mix_own, mix_sib, first_in, cot_second, sib_rows, par, bias_inner, gathered
    )
    back_sib = swap(back)
    grad_first, branch, g0, g1, g2, g3, norm_sums = first_back(
        where, back, back_sib, first_sum, cot_first, sib_rows, par, gathered
    )
    grad_mixed = jnp.concatenate(scatter([g0, g1, g2, g3], "z"))
    grad_inner, grad_outer, grad_output, second_own, second_give, cot_sum = weight_grads(
        where, active, grad_hidden, input_t, cot_second, sib_rows, mix_own, mix_sib, branch,
        gathered,
    )
    second_out = (
        second_in.astype(F32) + second_own + swap(second_give) + par[4]
    ).astype(BF)

    grad_inner = grad_inner.reshape(4, 4, 4, 16, 2048)
    grad_outer = grad_outer.reshape(4, 4, 4, 32, D)
    grad_output = grad_output.reshape(4, 4, 4, 16, 512)
    sums = jnp.stack([norm_sums[0], norm_sums[1], cot_sum[0]]).reshape(3, 64, 16)
    sums = jnp.pad(jnp.transpose(sums, (1, 0, 2)), ((0, 0), (0, 0), (0, 16)))
    sums = jnp.concatenate([sums, hid_sum[0].reshape(64, 1, 32)], axis=1).astype(BF)
    sums = jnp.pad(sums, ((0, 0), (0, 4), (0, D - 32))).reshape(4, 4, 4, 8, D)
    part_a = grad_inner[..., :1536]
    part_b = grad_outer[:, :, :, :24]
    part_c = jnp.concatenate(
        [
            jnp.concatenate([grad_inner[..., 1536:], grad_output], axis=4),
            grad_outer[:, :, :, 24:],
            sums,
        ],
        axis=3,
    )
    part_a = reduce_chips(part_a, ("x", "y", "z"))
    part_b = reduce_chips(part_b, ("y", "z", "x"))
    part_c = reduce_chips(part_c, ("z", "x", "y"))
    grad_outer = jnp.concatenate([part_b, part_c[16:24]], axis=0)
    inner_sum = jnp.concatenate([part_a, part_c[:16, :512]], axis=1).astype(BF)
    output_sum = part_c[:16, 512:].astype(BF)
    chip_sum = jnp.concatenate([inner_sum, output_sum], axis=1)
    rows_keep = by_core(chip_sum[:8], chip_sum[8:])
    rows_got = swap(by_core(chip_sum[8:], chip_sum[:8]))
    rows_low = by_core(rows_keep, rows_got)
    rows_high = by_core(rows_got, rows_keep)
    grad_inner = jnp.stack(
        [rows_low[:, :2048].reshape(8, 64, 32), rows_high[:, :2048].reshape(8, 64, 32)], axis=2
    ).reshape(8, FF).astype(F32)
    grad_output = jnp.concatenate([rows_low[:, 2048:], rows_high[:, 2048:]], axis=1).astype(F32)
    small = part_c[24:28, :32]
    mine16 = by_core(small[:3, :8], small[:3, 8:16])
    grad_ffn_gain, grad_ffn_shift, grad_b_outer = mine16[0], mine16[1], mine16[2]
    grad_b_inner = small[3]

    gq, gkv = attend_back(tgt, tgt_t, mask, kv, qm, round_out, round_total, grad_mixed)
    gkv_got = scatter([gkv[m] for m in range(4)], "x")
    back_own, back_give, w_grad = project_back(
        where, tokens, par, w_qv, normed, qv, gq, gkv_got
    )
    back_chip = (back_own.astype(F32) + swap(back_give).astype(F32)).astype(BF)
    back_parts = scatter([back_chip[k] for k in range(4)], "z")
    grad_normed = back_parts[0].astype(F32)
    for part in back_parts[1:]:
        grad_normed = grad_normed + part.astype(F32)
    attn_xhat, attn_scale = normalized(second_in.astype(F32))
    attn_back = norm_back(grad_normed * par[0], attn_xhat, attn_scale)
    grad_second = (cot_second.astype(F32) + attn_back).astype(BF)

    w_grad = w_grad.reshape(4, 4, 4, 2, 8, 384)
    w_grad = reduce_over(w_grad, "y", 0).astype(BF)
    w_grad = reduce_over(w_grad, "x", 1).astype(BF)
    w_rows = [
        lax.dynamic_index_in_dim(w_grad, (z + k) % 4, 0, keepdims=False) for k in range(4)
    ]
    w_rows = in_order(scatter(w_rows, "z"), z)
    rows_keep = by_core(w_rows[:, 0], w_rows[:, 1])
    rows_got = swap(by_core(w_rows[:, 1], w_rows[:, 0]))
    heads = by_core(
        jnp.concatenate([rows_keep, rows_got]), jnp.concatenate([rows_got, rows_keep])
    ).astype(F32)
    grad_joint = jnp.transpose(heads[:, :, :128], (1, 0, 2)).reshape(8, D)
    grad_value = jnp.transpose(heads[:, :, 128:256], (1, 0, 2)).reshape(8, D)
    grad_attn_gain = jnp.sum(heads[:, :, 256], axis=0)
    grad_attn_shift = jnp.sum(heads[:, :, 320], axis=0)

    return (
        first_out, second_out, grad_first, grad_second, grad_attn_gain, grad_attn_shift,
        grad_joint, grad_value, grad_output, grad_ffn_gain, grad_ffn_shift, grad_inner,
        grad_b_inner, grad_outer, grad_b_outer,
    )


def solution(mesh):
    chips = Mesh(mesh.devices.reshape(4, 4, 4, 2), AXES)
    rows, flat = P(AXES, None), P(AXES)
    return jax.shard_map(
        local,
        mesh=chips,
        in_specs=(
            rows, rows, flat, flat, rows, rows, rows, flat, flat, rows, flat, rows, flat,
            P(None, AXES, None), rows, rows,
        ),
        out_specs=(
            rows, rows, rows, rows, flat, flat, rows, rows, rows, flat, flat, rows, flat, rows,
            flat,
        ),
        check_vma=False,
    )
```

time: 3670 us -> 505 us (0.14)
  waiting for transfers between devices: 3160 us -> 202 us
  blocking collectives: 244 us -> 0 us
  matrix products: 130 us -> 0 us
  Pallas kernels: 0 us -> 109 us
  starting transfers between devices: 29.8 us -> 113 us
    reduce_scatter x5 -> x0, waiting for transfers between devices: 2960 us -> none  [the longest x1 662 us: local(): lax.psum_scatter(grad_outer, ('dp', 'seq'), scatter_dimension=0, tiled=True)]
    ppermute x0 -> x73, waiting for transfers between devices: none -> 202 us  [the longest x63 199 us: send(): return lax.ppermute(piece, axis, [(i, (i + k) % 4) for i in range(4)])]
    all_gather x5 -> x1, waiting for transfers between devices: 150 us -> 0.01 us  [local(): lax.all_gather(payload(where, keep_b, got_b, w_outer)[0], CHIPS, axis=0,...]
    unnamed x2 -> x0, blocking collectives: 134 us -> none
    dot_general x27 -> x0, matrix products: 130 us -> none  [the longest x1 18.2 us: owner_backward(): jnp.einsum('rhqk,rkhd->rqhd', grad_scores, key_rows, preferred_element_ty...]
    ppermute x0 -> x73, starting transfers between devices: none -> 112 us  [the longest x63 111 us: send(): return lax.ppermute(piece, axis, [(i, (i + k) % 4) for i in range(4)])]
    all_to_all x4 -> x0, blocking collectives: 111 us -> none  [the longest x1 34.2 us: local(): lax.all_to_all(sent_grads[0], 'seq', split_axis=1, concat_axis=1, tiled=T...]
    pallas_call x0 -> x12, Pallas kernels: none -> 109 us  [the longest x1 36.5 us: attend_back(): pl.pallas_call(attend_back_kernel, grid=(ROUNDS,), in_specs=[per_round((3...]
  transfers between devices with their start and end apart: 15 -> 74, of which waited for: 10 -> 33; matrix products, arithmetic and copies ran while one was open for 5% -> 6% of each run, Pallas kernels for 0% -> 11%
where the time goes in v1:
time: 505 us; the launch traced here: 495 us
  waiting for transfers between devices  202 us (40%)
  starting transfers between devices  113 us (22%)
  Pallas kernels  109 us (22%)
  local copies, waits for them, and re-layouts  41.2 us (8%)
  between operations  15.6 us (3%)
  other arithmetic  14.2 us (3%)
    ppermute x63, waiting for transfers between devices, send(): return lax.ppermute(piece, axis, [(i, (i + k) % 4) for i in range(4)])  199 us
    ppermute x63, starting transfers between devices, send(): return lax.ppermute(piece, axis, [(i, (i + k) % 4) for i in range(4)])  111 us
    pallas_call x1, Pallas kernels, attend_back(): pl.pallas_call(attend_back_kernel, grid=(ROUNDS,), in_specs=[per_round((3...  36.5 us
    pallas_call x1, Pallas kernels, attend(): pl.pallas_call(attend_kernel, grid=(ROUNDS,), in_specs=[fixed((rows, 256)...  21.7 us
    unnamed x109, local copies, waits for them, and re-layouts  19.4 us
    pallas_call x1, Pallas kernels, feed(): pl.pallas_call(feed_kernel, grid=(8,), in_specs=[SMEM, pl.BlockSpec((two,...  14 us
  transfers between devices with their start and end apart: 74, of which 33 were waited for; matrix products, arithmetic and copies ran while one was open for 6% of the time, Pallas kernels for 11%

profile of v1, /device:TPU:0, one launch (start us, length us, event | category | flops | bytes accessed | tf_op | source)
XLA Modules:
  0.0 495.0 jit_solution(13540477934669070588)
XLA Ops:
  19.5 3.6 collective-permute-start.1
  27.9 7.6 %collective-permute-done.6 = bf16[64,128]{1,0:T(8,128)(2,1)S(1)} collective-permute-done((bf16[64,128]{1,0:T(8,128)(2,1)S(1)}, bf16[64,128]{1,0:T(8,128)(2,1)S(1)}, u32[]{:S(2)}, u32[]{:S(2)}) %collective-permute-start.6) | collective-permute-done | bytes 16416 | tf_op jit(solution)/shard_map/ppermute | solution.py:30
  35.6 2.8 collective-permute-start.7
  38.4 2.4 collective-permute-done.7
  40.9 3.1 collective-permute-start.9
  45.7 2.5 collective-permute-start.10
  48.2 3.1 collective-permute-done.10
  52.2 5.0 %collective-permute-done.11 = bf16[192,128]{1,0:T(8,128)(2,1)S(1)} collective-permute-done((bf16[192,128]{1,0:T(8,128)(2,1)S(1)}, bf16[192,128]{1,0:T(8,128)(2,1)S(1)}, u32[]{:S(2)}, u32[]{:S(2)}) %collective-permute-start.11) | collective-permute-done | bytes 49184 | tf_op jit(solution)/shard_map/ppermute | solution.py:30
  57.5 2.8 collective-permute-start.12
  62.0 9.7 %collective-permute-done.12.x1 = bf16[832,128]{1,0:T(8,128)(2,1)S(1)} collective-permute-done((bf16[832,128]{1,0:T(8,128)(2,1)S(1)}, bf16[832,128]{1,0:T(8,128)(2,1)S(1)}, u32[]{:S(2)}, u32[]{:S(2)}) %collective-permute-start.12) | collective-permute-done | bytes 213024 | tf_op jit(solution)/shard_map/ppermute | solution.py:30
  71.7 3.5 collective-permute-done.14.x3
  76.3 4.6 project.1
  83.2 5.1 %make_mask.1.mask_ref = bf16[4,16,256,128]{3,2,1,0:T(8,128)(2,1)S(1)} custom-call(s32[4]{0:T(128)S(1)} %pad_add_fusion.where, f32[4,32,128]{2,1,0:T(8,128)S(1)} %get-tuple-element.71.count_ref), custom_call_target="tpu_custom_call" | custom-call | flops 6000000000 | tf_op jit(solution)/shard_map/make_mask/pallas_call | solution.py:300
  88.3 18.7 %collective-permute-done.15.p1 = bf16[1024,256]{1,0:T(8,128)(2,1)S(1)} collective-permute-done((bf16[1024,256]{1,0:T(8,128)(2,1)S(1)}, bf16[1024,256]{1,0:T(8,128)(2,1)S(1)}, u32[]{:S(2)}, u32[]{:S(2)}) %collective-permute-start.15) | collective-permute-done | bytes 524320 | tf_op jit(solution)/shard_map/ppermute | solution.py:30
  109.3 17.0 %collective-permute-done.17.p3 = bf16[1024,256]{1,0:T(8,128)(2,1)S(1)} collective-permute-done((bf16[1024,256]{1,0:T(8,128)(2,1)S(1)}, bf16[1024,256]{1,0:T(8,128)(2,1)S(1)}, u32[]{:S(2)}, u32[]{:S(2)}) %collective-permute-start.17) | collective-permute-done | bytes 524320 | tf_op jit(solution)/shard_map/ppermute | solution.py:30
  126.3 21.7 %attend.1 = (bf16[1024,128]{1,0:T(8,128)(2,1)S(1)}, bf16[4,1024,128]{2,1,0:T(8,128)(2,1)S(1)}, bf16[4,1024,128]{2,1,0:T(8,128)(2,1)S(1)}, bf16[4,16,256,512]{3,2,1,0:T(8,128)(2,1)}, bf16[4,16,128,256]{3,2,1,0:T(8,128)(2,1)S(1)}) custom-call(bf16[1024,256]{1,0:T(8,128)(2,1)S(1)} %get-tuple-element.68.p0.qv_ref, ...), custom_call_target="tpu_custom_call" | custom-call | flops 24000000000 | tf_op jit(solution)/shard_map/attend/pallas_call | solution.py:834
  153.5 2.8 collective-permute-start.19
  169.1 14.0 %feed.1 = (f32[256,1024]{1,0:T(8,128)S(1)}, bf16[128,1024]{1,0:T(8,128)(2,1)}, bf16[1024,256]{1,0:T(8,128)(2,1)S(1)}, bf16[256,2048]{1,0:T(8,128)(2,1)S(1)}, bf1...) custom-call(s32[4]{0:T(128)S(1)} %pad_add_fusion.where, ...), custom_call_target="tpu_custom_call" | custom-call | flops 16000000000 | tf_op jit(solution)/shard_map/feed/pallas_call | solution.py:532
  191.1 4.3 first_back.1
  195.9 3.6 collective-permute-start.26
  200.9 10.0 %weight_grads.1 = (bf16[64,16,2048]{2,1,0:T(8,128)(2,1)S(1)}, bf16[64,32,1024]{2,1,0:T(8,128)(2,1)}, bf16[64,16,512]{2,1,0:T(8,128)(2,1)S(1)}, f32[128,1024]{1,0...) custom-call(s32[4]{0:T(128)S(1)} %pad_add_fusion.where, bf16[256,2048]{1,0:T(8,128)(2,1)S(1)} %copy-done.27, ...), custom_call_target="tpu_custom_call" | custom-call | flops 14000000000 | tf_op jit(solution)/shard_map/weight_grads/pallas_call | solution.py:661
  214.9 36.5 %attend_back.1 = (f32[1024,128]{1,0:T(8,128)}, bf16[4,1024,256]{2,1,0:T(8,128)(2,1)}) custom-call(s32[4,32,128]{2,1,0:T(8,128)} %copy-done.30, s32[4,128,128]{2,1,0:T(8,128)} %copy-done.25, bf16[4,16,256,128]{3,2,1,0:T(8,128)(2,1)} %copy-done.22, bf16[4,16,256,512]{3,2,1,0:T(8,128)(2,1)} %get-tuple-element.86.kv_ref, bf16[4,16,128,256]{3,2,1,0:T(8,128)(2,1)} %copy-done.34, ...), custom_call_target="tpu_custom_call" | custom-call | flops 38000001024 | tf_op jit(solution)/shard_map/attend_back/pallas_call | solution.py:938
  251.4 2.7 slice_bitcast_fusion
  254.1 5.1 %collective-permute-start.28 = (bf16[1024,256]{1,0:T(8,128)(2,1)}, bf16[1024,256]{1,0:T(8,128)(2,1)}, u32[]{:S(2)}, u32[]{:S(2)}) collective-permute-start(bf16[1024,256]{1,0:T(8,128)(2,1)} %get-tuple-element.122), channel_id=1, source_target_pairs={{0,6},{2,0},{4,2},{6,4},{1,7},{3,1},{5,3},{7,5},{8,14},{10,8},{12,... | collective-permute-start | bytes 1572872 | tf_op jit(solution)/shard_map/ppermute | solution.py:30
  263.8 2.7 collective-permute-start.47
  267.7 31.0 %collective-permute-done.28.g1 = bf16[1024,256]{1,0:T(8,128)(2,1)} collective-permute-done((bf16[1024,256]{1,0:T(8,128)(2,1)}, bf16[1024,256]{1,0:T(8,128)(2,1)}, u32[]{:S(2)}, u32[]{:S(2)}) %collective-permute-start.28) | collective-permute-done | bytes 524320 | tf_op jit(solution)/shard_map/ppermute | solution.py:30
  298.8 3.9 collective-permute-start.45
  302.7 9.4 %project_back.1 = (bf16[4,128,1024]{2,1,0:T(8,128)(2,1)S(1)}, bf16[4,128,1024]{2,1,0:T(8,128)(2,1)S(1)}, bf16[1024,384]{1,0:T(8,128)(2,1)S(1)}) custom-call(s32[4]{0:T(128)S(1)} %pad_add_fusion.where, bf16[128,1024]{1,0:T(8,128)(2,1)S(1)} %copy-done, bf16[3,128,1024]{2,1,0:T(8,128)(2,1)S(1)} %pad_maximum_fusion.2.own3, bf16[4,128,1024]{2,1,0:T(8,128)(2,1)S(1)} %copy-done.6, ...), custom_call_target="tpu_custom_call" | custom-call | flops 8000000000 | tf_op jit(solution)/shard_map/project_back/pallas_call | solution.py:416
  312.8 3.1 collective-permute-start.36
  316.0 7.2 %collective-permute-done.37 = bf16[4,4,2,8,384]{4,3,2,1,0:T(8,128)(2,1)S(1)} collective-permute-done((bf16[4,4,2,8,384]{4,3,2,1,0:T(8,128)(2,1)S(1)}, bf16[4,4,2,8,384]{4,3,2,1,0:T(8,128)(2,1)S(1)}, u32[]{:S(2)}, u32[]{:S(2)}) %collective-permute-start.37) | collective-permute-done | bytes 196640 | tf_op jit(solution)/shard_map/ppermute | solution.py:30
  327.8 2.4 collective-permute-done.35
  335.6 13.2 %collective-permute-done.66 = bf16[4,4,24,1024]{3,2,1,0:T(8,128)(2,1)S(1)} collective-permute-done((bf16[4,4,24,1024]{3,2,1,0:T(8,128)(2,1)S(1)}, bf16[4,4,24,1024]{3,2,1,0:T(8,128)(2,1)S(1)}, u32[]{:S(2)}, u32[]{:S(2)}) %collective-permute-start.66) | collective-permute-done | bytes 786464 | tf_op jit(solution)/shard_map/ppermute | solution.py:30
  348.8 12.2 %collective-permute-done.65 = bf16[4,4,24,1024]{3,2,1,0:T(8,128)(2,1)S(1)} collective-permute-done((bf16[4,4,24,1024]{3,2,1,0:T(8,128)(2,1)S(1)}, bf16[4,4,24,1024]{3,2,1,0:T(8,128)(2,1)S(1)}, u32[]{:S(2)}, u32[]{:S(2)}) %collective-permute-start.65) | collective-permute-done | bytes 786464 | tf_op jit(solution)/shard_map/ppermute | solution.py:30
  370.8 4.3 collective-permute-done.42
  376.7 3.3 collective-permute-done.43
  387.4 3.2 collective-permute-start.49
  391.6 3.5 collective-permute-done.49
  395.1 3.6 collective-permute-done.48
  398.8 18.9 %collective-permute-start.53 = (bf16[16,1536]{1,0:T(8,128)(2,1)S(1)}, bf16[16,1536]{1,0:T(8,128)(2,1)S(1)}, u32[]{:S(2)}, u32[]{:S(2)}) collective-permute-start(bf16[16,1536]{1,0:T(8,128)(2,1)S(1)} %get-tuple-element.152), channel_id=1, source_target_pairs={{0,8},{8,16},{16,24},{24,0},{1,9},{9,17},{17,25},{25,1},{2,10},{10... | collective-permute-start | bytes 147464 | tf_op jit(solution)/shard_map/ppermute | solution.py:30
  417.7 16.1 %collective-permute-done.54 = bf16[4,4,32,1024]{3,2,0,1:T(8,128)(2,1)S(1)} collective-permute-done((bf16[4,4,32,1024]{3,2,0,1:T(8,128)(2,1)S(1)}, bf16[4,4,32,1024]{3,2,0,1:T(8,128)(2,1)S(1)}, u32[]{:S(2)}, u32[]{:S(2)}) %collective-permute-start.54) | collective-permute-done | bytes 1048608 | tf_op jit(solution)/shard_map/ppermute | solution.py:30
  436.8 2.8 collective-permute-start.58
  440.1 10.9 %collective-permute-done.59 = bf16[4,32,1024]{2,1,0:T(8,128)(2,1)S(1)} collective-permute-done((bf16[4,32,1024]{2,1,0:T(8,128)(2,1)S(1)}, bf16[4,32,1024]{2,1,0:T(8,128)(2,1)S(1)}, u32[]{:S(2)}, u32[]{:S(2)}) %collective-permute-start.59) | collective-permute-done | bytes 262176 | tf_op jit(solution)/shard_map/ppermute | solution.py:30
  452.0 2.4 collective-permute-start.70
  454.6 2.3 collective-permute-done.72
  457.2 3.0 collective-permute-start.61
  460.2 2.3 collective-permute-start.60
  469.4 2.3 collective-permute-start.32
  474.6 9.0 %collective-permute-done.34 = bf16[128,1024]{1,0:T(8,128)(2,1)} collective-permute-done((bf16[128,1024]{1,0:T(8,128)(2,1)}, bf16[128,1024]{1,0:T(8,128)(2,1)}, u32[]{:S(2)}, u32[]{:S(2)}) %collective-permute-start.34) | collective-permute-done | bytes 262176 | tf_op jit(solution)/shard_map/ppermute | solution.py:30
  (317 shorter events, 114.2 us)
Async XLA Ops:
  7.2 160.9 %all-gather.3.cloned.1.call-start = ((), (), s32[]{:S(2)}) async-start(), calls=%async_computation | async-start | bytes 10649600 | tf_op jit(solution)/shard_map/all_gather | solution.py:994
  17.5 39.8 %collective-permute-start.2 = (bf16[128,1024]{1,0:T(8,128)(2,1)S(1)}, bf16[128,1024]{1,0:T(8,128)(2,1)S(1)}, u32[]{:S(2)}, u32[]{:S(2)}) collective-permute-start(bf16[128,1024]{1,0:T(8,128)(2,1)S(1)} %copy-done), channel_id=1, source_target_pairs={{0,8},{8,16},{16,24},{24,0},{1,9},{9,17},{17,25},{25,1},{2,10},{10... | collective-permute-start | bytes 786440 | tf_op jit(solution)/shard_map/ppermute | solution.py:30
  19.5 37.8 %collective-permute-start.1 = (bf16[128,1024]{1,0:T(8,128)(2,1)S(1)}, bf16[128,1024]{1,0:T(8,128)(2,1)S(1)}, u32[]{:S(2)}, u32[]{:S(2)}) collective-permute-start(bf16[128,1024]{1,0:T(8,128)(2,1)S(1)} %copy-done), channel_id=1, source_target_pairs={{0,16},{8,24},{16,0},{24,8},{1,17},{9,25},{17,1},{25,9},{2,18},{10... | collective-permute-start | bytes 786440 | tf_op jit(solution)/shard_map/ppermute | solution.py:30
  23.1 34.2 %collective-permute-start = (bf16[128,1024]{1,0:T(8,128)(2,1)S(1)}, bf16[128,1024]{1,0:T(8,128)(2,1)S(1)}, u32[]{:S(2)}, u32[]{:S(2)}) collective-permute-start(bf16[128,1024]{1,0:T(8,128)(2,1)S(1)} %copy-done), channel_id=1, source_target_pairs={{0,24},{8,0},{16,8},{24,16},{1,25},{9,1},{17,9},{25,17},{2,26},{10... | collective-permute-start | bytes 786440 | tf_op jit(solution)/shard_map/ppermute | solution.py:30
  24.6 16.2 %collective-permute-start.8 = (bf16[64,128]{1,0:T(8,128)(2,1)S(1)}, bf16[64,128]{1,0:T(8,128)(2,1)S(1)}, u32[]{:S(2)}, u32[]{:S(2)}) collective-permute-start(bf16[64,128]{1,0:T(8,128)(2,1)S(1)} %get-tuple-element.65), channel_id=1, source_target_pairs={{0,8},{8,16},{16,24},{24,0},{1,9},{9,17},{17,25},{25,1},{2,10},{10... | collective-permute-start | bytes 49160 | tf_op jit(solution)/shard_map/ppermute | solution.py:30
  25.7 9.8 %collective-permute-start.6 = (bf16[64,128]{1,0:T(8,128)(2,1)S(1)}, bf16[64,128]{1,0:T(8,128)(2,1)S(1)}, u32[]{:S(2)}, u32[]{:S(2)}) collective-permute-start(bf16[64,128]{1,0:T(8,128)(2,1)S(1)} %get-tuple-element.63), channel_id=1, source_target_pairs={{0,24},{8,0},{16,8},{24,16},{1,25},{9,1},{17,9},{25,17},{2,26},{10... | collective-permute-start | bytes 49160 | tf_op jit(solution)/shard_map/ppermute | solution.py:30
  44.1 32.2 %collective-permute-start.3 = (bf16[4,128,1024]{2,1,0:T(8,128)(2,1)S(1)}, bf16[4,128,1024]{2,1,0:T(8,128)(2,1)S(1)}, u32[]{:S(2)}, u32[]{:S(2)}) collective-permute-start(bf16[4,128,1024]{2,1,0:T(8,128)(2,1)S(1)} %pad_maximum_fusion.1), channel_id=1, source_target_pairs={{0,1},{1,0},{2,3},{3,2},{4,5},{5,4},{6,7},{7,6},{8,9},{9,8},{10,11... | collective-permute-start | bytes 3145736 | tf_op jit(solution)/shard_map/ppermute | solution.py:34
  57.4 18.9 %collective-permute-start.4 = (bf16[3,128,1024]{2,1,0:T(8,128)(2,1)S(1)}, bf16[3,128,1024]{2,1,0:T(8,128)(2,1)S(1)}, u32[]{:S(2)}, u32[]{:S(2)}) collective-permute-start(bf16[3,128,1024]{2,1,0:T(8,128)(2,1)S(1)} %pad_maximum_fusion.2.own3), channel_id=1, source_target_pairs={{0,1},{1,0},{2,3},{3,2},{4,5},{5,4},{6,7},{7,6},{8,9},{9,8},{10,11... | collective-permute-start | bytes 2359304 | tf_op jit(solution)/shard_map/ppermute | solution.py:34
  57.5 14.2 %collective-permute-start.12 = (bf16[832,128]{1,0:T(8,128)(2,1)S(1)}, bf16[832,128]{1,0:T(8,128)(2,1)S(1)}, u32[]{:S(2)}, u32[]{:S(2)}) collective-permute-start(bf16[832,128]{1,0:T(8,128)(2,1)S(1)} %constant_dynamic-update-slice_fusion.8.x0), channel_id=1, source_target_pairs={{0,6},{2,0},{4,2},{6,4},{1,7},{3,1},{5,3},{7,5},{8,14},{10,8},{12,... | collective-permute-start | bytes 638984 | tf_op jit(solution)/shard_map/ppermute | solution.py:30
  60.3 11.4 %collective-permute-start.13 = (bf16[832,128]{1,0:T(8,128)(2,1)S(1)}, bf16[832,128]{1,0:T(8,128)(2,1)S(1)}, u32[]{:S(2)}, u32[]{:S(2)}) collective-permute-start(bf16[832,128]{1,0:T(8,128)(2,1)S(1)} %constant_dynamic-update-slice_fusion.8.x0), channel_id=1, source_target_pairs={{0,4},{2,6},{4,0},{6,2},{1,5},{3,7},{5,1},{7,3},{8,12},{10,14},{12... | collective-permute-start | bytes 638984 | tf_op jit(solution)/shard_map/ppermute | solution.py:30
  61.1 14.1 %collective-permute-start.14 = (bf16[832,128]{1,0:T(8,128)(2,1)S(1)}, bf16[832,128]{1,0:T(8,128)(2,1)S(1)}, u32[]{:S(2)}, u32[]{:S(2)}) collective-permute-start(bf16[832,128]{1,0:T(8,128)(2,1)S(1)} %constant_dynamic-update-slice_fusion.8.x0), channel_id=1, source_target_pairs={{0,2},{2,4},{4,6},{6,0},{1,3},{3,5},{5,7},{7,1},{8,10},{10,12},{12... | collective-permute-start | bytes 638984 | tf_op jit(solution)/shard_map/ppermute | solution.py:30
  81.0 26.1 %collective-permute-start.15 = (bf16[1024,256]{1,0:T(8,128)(2,1)S(1)}, bf16[1024,256]{1,0:T(8,128)(2,1)S(1)}, u32[]{:S(2)}, u32[]{:S(2)}) collective-permute-start(bf16[1024,256]{1,0:T(8,128)(2,1)S(1)} %get-tuple-element.68.p0.qv_ref), channel_id=1, source_target_pairs={{0,6},{2,0},{4,2},{6,4},{1,7},{3,1},{5,3},{7,5},{8,14},{10,8},{12,... | collective-permute-start | bytes 1572872 | tf_op jit(solution)/shard_map/ppermute | solution.py:30
  81.8 27.5 %collective-permute-start.16 = (bf16[1024,256]{1,0:T(8,128)(2,1)S(1)}, bf16[1024,256]{1,0:T(8,128)(2,1)S(1)}, u32[]{:S(2)}, u32[]{:S(2)}) collective-permute-start(bf16[1024,256]{1,0:T(8,128)(2,1)S(1)} %get-tuple-element.68.p0.qv_ref), channel_id=1, source_target_pairs={{0,4},{2,6},{4,0},{6,2},{1,5},{3,7},{5,1},{7,3},{8,12},{10,14},{12... | collective-permute-start | bytes 1572872 | tf_op jit(solution)/shard_map/ppermute | solution.py:30
  82.3 43.9 %collective-permute-start.17 = (bf16[1024,256]{1,0:T(8,128)(2,1)S(1)}, bf16[1024,256]{1,0:T(8,128)(2,1)S(1)}, u32[]{:S(2)}, u32[]{:S(2)}) collective-permute-start(bf16[1024,256]{1,0:T(8,128)(2,1)S(1)} %get-tuple-element.68.p0.qv_ref), channel_id=1, source_target_pairs={{0,2},{2,4},{4,6},{6,0},{1,3},{3,5},{5,7},{7,1},{8,10},{10,12},{12... | collective-permute-start | bytes 1572872 | tf_op jit(solution)/shard_map/ppermute | solution.py:30
  195.4 18.8 %collective-permute-start.27 = (bf16[256,128]{1,0:T(8,128)(2,1)S(1)}, bf16[256,128]{1,0:T(8,128)(2,1)S(1)}, u32[]{:S(2)}, u32[]{:S(2)}) collective-permute-start(bf16[256,128]{1,0:T(8,128)(2,1)S(1)} %get-tuple-element.93), channel_id=1, source_target_pairs={{0,8},{8,16},{16,24},{24,0},{1,9},{9,17},{17,25},{25,1},{2,10},{10... | collective-permute-start | bytes 196616 | tf_op jit(solution)/shard_map/ppermute | solution.py:30
  195.9 18.3 %collective-permute-start.26 = (bf16[256,128]{1,0:T(8,128)(2,1)S(1)}, bf16[256,128]{1,0:T(8,128)(2,1)S(1)}, u32[]{:S(2)}, u32[]{:S(2)}) collective-permute-start(bf16[256,128]{1,0:T(8,128)(2,1)S(1)} %get-tuple-element.92), channel_id=1, source_target_pairs={{0,16},{8,24},{16,0},{24,8},{1,17},{9,25},{17,1},{25,9},{2,18},{10... | collective-permute-start | bytes 196616 | tf_op jit(solution)/shard_map/ppermute | solution.py:30
  199.5 14.7 %collective-permute-start.25 = (bf16[256,128]{1,0:T(8,128)(2,1)S(1)}, bf16[256,128]{1,0:T(8,128)(2,1)S(1)}, u32[]{:S(2)}, u32[]{:S(2)}) collective-permute-start(bf16[256,128]{1,0:T(8,128)(2,1)S(1)} %get-tuple-element.91), channel_id=1, source_target_pairs={{0,24},{8,0},{16,8},{24,16},{1,25},{9,1},{17,9},{25,17},{2,26},{10... | collective-permute-start | bytes 196616 | tf_op jit(solution)/shard_map/ppermute | solution.py:30
  254.1 44.7 %collective-permute-start.28 = (bf16[1024,256]{1,0:T(8,128)(2,1)}, bf16[1024,256]{1,0:T(8,128)(2,1)}, u32[]{:S(2)}, u32[]{:S(2)}) collective-permute-start(bf16[1024,256]{1,0:T(8,128)(2,1)} %get-tuple-element.122), channel_id=1, source_target_pairs={{0,6},{2,0},{4,2},{6,4},{1,7},{3,1},{5,3},{7,5},{8,14},{10,8},{12,... | collective-permute-start | bytes 1572872 | tf_op jit(solution)/shard_map/ppermute | solution.py:30
  259.2 43.4 %collective-permute-start.29 = (bf16[1024,256]{1,0:T(8,128)(2,1)}, bf16[1024,256]{1,0:T(8,128)(2,1)}, u32[]{:S(2)}, u32[]{:S(2)}) collective-permute-start(bf16[1024,256]{1,0:T(8,128)(2,1)} %get-tuple-element.121), channel_id=1, source_target_pairs={{0,4},{2,6},{4,0},{6,2},{1,5},{3,7},{5,1},{7,3},{8,12},{10,14},{12... | collective-permute-start | bytes 1572872 | tf_op jit(solution)/shard_map/ppermute | solution.py:30
  259.2 43.4 %collective-permute-start.30 = (bf16[1024,256]{1,0:T(8,128)(2,1)}, bf16[1024,256]{1,0:T(8,128)(2,1)}, u32[]{:S(2)}, u32[]{:S(2)}) collective-permute-start(bf16[1024,256]{1,0:T(8,128)(2,1)} %get-tuple-element.120), channel_id=1, source_target_pairs={{0,2},{2,4},{4,6},{6,0},{1,3},{3,5},{5,7},{7,1},{8,10},{10,12},{12... | collective-permute-start | bytes 1572872 | tf_op jit(solution)/shard_map/ppermute | solution.py:30
  263.8 66.6 %collective-permute-start.47 = (bf16[4,4,16,1536]{3,2,1,0:T(8,128)(2,1)S(1)}, bf16[4,4,16,1536]{3,2,1,0:T(8,128)(2,1)S(1)}, u32[]{:S(2)}, u32[]{:S(2)}) collective-permute-start(bf16[4,4,16,1536]{3,2,1,0:T(8,128)(2,1)S(1)} %get-tuple-element.119), channel_id=1, source_target_pairs={{0,2},{2,4},{4,6},{6,0},{1,3},{3,5},{5,7},{7,1},{8,10},{10,12},{12... | collective-permute-start | bytes 2359304 | tf_op jit(solution)/shard_map/ppermute | solution.py:30
  266.5 65.2 %collective-permute-start.46 = (bf16[4,4,16,1536]{3,2,1,0:T(8,128)(2,1)S(1)}, bf16[4,4,16,1536]{3,2,1,0:T(8,128)(2,1)S(1)}, u32[]{:S(2)}, u32[]{:S(2)}) collective-permute-start(bf16[4,4,16,1536]{3,2,1,0:T(8,128)(2,1)S(1)} %get-tuple-element.118), channel_id=1, source_target_pairs={{0,4},{2,6},{4,0},{6,2},{1,5},{3,7},{5,1},{7,3},{8,12},{10,14},{12... | collective-permute-start | bytes 2359304 | tf_op jit(solution)/shard_map/ppermute | solution.py:30
  298.8 35.1 %collective-permute-start.45 = (bf16[4,4,16,1536]{3,2,1,0:T(8,128)(2,1)S(1)}, bf16[4,4,16,1536]{3,2,1,0:T(8,128)(2,1)S(1)}, u32[]{:S(2)}, u32[]{:S(2)}) collective-permute-start(bf16[4,4,16,1536]{3,2,1,0:T(8,128)(2,1)S(1)} %get-tuple-element.117), channel_id=1, source_target_pairs={{0,6},{2,0},{4,2},{6,4},{1,7},{3,1},{5,3},{7,5},{8,14},{10,8},{12,... | collective-permute-start | bytes 2359304 | tf_op jit(solution)/shard_map/ppermute | solution.py:30
  312.2 10.9 %collective-permute-start.37 = (bf16[4,4,2,8,384]{4,3,2,1,0:T(8,128)(2,1)S(1)}, bf16[4,4,2,8,384]{4,3,2,1,0:T(8,128)(2,1)S(1)}, u32[]{:S(2)}, u32[]{:S(2)}) collective-permute-start(bf16[4,4,2,8,384]{4,3,2,1,0:T(8,128)(2,1)S(1)} %get-tuple-element.137), channel_id=1, source_target_pairs={{0,32},{32,64},{64,96},{96,0},{1,33},{33,65},{65,97},{97,1},{2,34}... | collective-permute-start | bytes 589832 | tf_op jit(solution)/shard_map/ppermute | solution.py:30
  312.8 13.5 %collective-permute-start.36 = (bf16[4,4,2,8,384]{4,3,2,1,0:T(8,128)(2,1)S(1)}, bf16[4,4,2,8,384]{4,3,2,1,0:T(8,128)(2,1)S(1)}, u32[]{:S(2)}, u32[]{:S(2)}) collective-permute-start(bf16[4,4,2,8,384]{4,3,2,1,0:T(8,128)(2,1)S(1)} %get-tuple-element.138), channel_id=1, source_target_pairs={{0,64},{32,96},{64,0},{96,32},{1,65},{33,97},{65,1},{97,33},{2,66}... | collective-permute-start | bytes 589832 | tf_op jit(solution)/shard_map/ppermute | solution.py:30
  326.3 72.5 %collective-permute-start.56 = (bf16[4,4,32,1024]{3,2,0,1:T(8,128)(2,1)S(1)}, bf16[4,4,32,1024]{3,2,0,1:T(8,128)(2,1)S(1)}, u32[]{:S(2)}, u32[]{:S(2)}) collective-permute-start(bf16[4,4,32,1024]{3,2,0,1:T(8,128)(2,1)S(1)} %bitcast.224), channel_id=1, source_target_pairs={{0,8},{8,16},{16,24},{24,0},{1,9},{9,17},{17,25},{25,1},{2,10},{10... | collective-permute-start | bytes 3145736 | tf_op jit(solution)/shard_map/ppermute | solution.py:30
  330.3 18.5 %collective-permute-start.66 = (bf16[4,4,24,1024]{3,2,1,0:T(8,128)(2,1)S(1)}, bf16[4,4,24,1024]{3,2,1,0:T(8,128)(2,1)S(1)}, u32[]{:S(2)}, u32[]{:S(2)}) collective-permute-start(bf16[4,4,24,1024]{3,2,1,0:T(8,128)(2,1)S(1)} %get-tuple-element.115), channel_id=1, source_target_pairs={{0,32},{32,64},{64,96},{96,0},{1,33},{33,65},{65,97},{97,1},{2,34}... | collective-permute-start | bytes 2359304 | tf_op jit(solution)/shard_map/ppermute | solution.py:30
  330.4 30.5 %collective-permute-start.65 = (bf16[4,4,24,1024]{3,2,1,0:T(8,128)(2,1)S(1)}, bf16[4,4,24,1024]{3,2,1,0:T(8,128)(2,1)S(1)}, u32[]{:S(2)}, u32[]{:S(2)}) collective-permute-start(bf16[4,4,24,1024]{3,2,1,0:T(8,128)(2,1)S(1)} %get-tuple-element.116), channel_id=1, source_target_pairs={{0,64},{32,96},{64,0},{96,32},{1,65},{33,97},{65,1},{97,33},{2,66}... | collective-permute-start | bytes 2359304 | tf_op jit(solution)/shard_map/ppermute | solution.py:30
  331.8 30.8 %collective-permute-start.64 = (bf16[4,4,24,1024]{3,2,1,0:T(8,128)(2,1)S(1)}, bf16[4,4,24,1024]{3,2,1,0:T(8,128)(2,1)S(1)}, u32[]{:S(2)}, u32[]{:S(2)}) collective-permute-start(bf16[4,4,24,1024]{3,2,1,0:T(8,128)(2,1)S(1)} %get-tuple-element.114), channel_id=1, source_target_pairs={{0,96},{32,0},{64,32},{96,64},{1,97},{33,1},{65,33},{97,65},{2,98}... | collective-permute-start | bytes 2359304 | tf_op jit(solution)/shard_map/ppermute | solution.py:30
  333.8 29.4 %collective-permute-start.40 = (bf16[4,2,8,384]{3,2,1,0:T(8,128)(2,1)S(1)}, bf16[4,2,8,384]{3,2,1,0:T(8,128)(2,1)S(1)}, u32[]{:S(2)}, u32[]{:S(2)}) collective-permute-start(bf16[4,2,8,384]{3,2,1,0:T(8,128)(2,1)S(1)} %get-tuple-element.155), channel_id=1, source_target_pairs={{0,2},{2,4},{4,6},{6,0},{1,3},{3,5},{5,7},{7,1},{8,10},{10,12},{12... | collective-permute-start | bytes 147464 | tf_op jit(solution)/shard_map/ppermute | solution.py:30
  348.8 14.5 %collective-permute-start.39 = (bf16[4,2,8,384]{3,2,1,0:T(8,128)(2,1)S(1)}, bf16[4,2,8,384]{3,2,1,0:T(8,128)(2,1)S(1)}, u32[]{:S(2)}, u32[]{:S(2)}) collective-permute-start(bf16[4,2,8,384]{3,2,1,0:T(8,128)(2,1)S(1)} %get-tuple-element.156), channel_id=1, source_target_pairs={{0,4},{2,6},{4,0},{6,2},{1,5},{3,7},{5,1},{7,3},{8,12},{10,14},{12... | collective-permute-start | bytes 147464 | tf_op jit(solution)/shard_map/ppermute | solution.py:30
  362.6 20.7 %collective-permute-start.50 = (bf16[4,16,1536]{2,1,0:T(8,128)(2,1)S(1)}, bf16[4,16,1536]{2,1,0:T(8,128)(2,1)S(1)}, u32[]{:S(2)}, u32[]{:S(2)}) collective-permute-start(bf16[4,16,1536]{2,1,0:T(8,128)(2,1)S(1)} %get-tuple-element.134), channel_id=1, source_target_pairs={{0,32},{32,64},{64,96},{96,0},{1,33},{33,65},{65,97},{97,1},{2,34}... | collective-permute-start | bytes 589832 | tf_op jit(solution)/shard_map/ppermute | solution.py:30
  365.8 19.3 %collective-permute-start.69 = (bf16[4,24,1024]{2,1,0:T(8,128)(2,1)S(1)}, bf16[4,24,1024]{2,1,0:T(8,128)(2,1)S(1)}, u32[]{:S(2)}, u32[]{:S(2)}) collective-permute-start(bf16[4,24,1024]{2,1,0:T(8,128)(2,1)S(1)} %get-tuple-element.131), channel_id=1, source_target_pairs={{0,8},{8,16},{16,24},{24,0},{1,9},{9,17},{17,25},{25,1},{2,10},{10... | collective-permute-start | bytes 589832 | tf_op jit(solution)/shard_map/ppermute | solution.py:30
  367.3 20.1 %collective-permute-start.68 = (bf16[4,24,1024]{2,1,0:T(8,128)(2,1)S(1)}, bf16[4,24,1024]{2,1,0:T(8,128)(2,1)S(1)}, u32[]{:S(2)}, u32[]{:S(2)}) collective-permute-start(bf16[4,24,1024]{2,1,0:T(8,128)(2,1)S(1)} %get-tuple-element.132), channel_id=1, source_target_pairs={{0,16},{8,24},{16,0},{24,8},{1,17},{9,25},{17,1},{25,9},{2,18},{10... | collective-permute-start | bytes 589832 | tf_op jit(solution)/shard_map/ppermute | solution.py:30
  381.3 9.2 %collective-permute-start.67 = (bf16[4,24,1024]{2,1,0:T(8,128)(2,1)S(1)}, bf16[4,24,1024]{2,1,0:T(8,128)(2,1)S(1)}, u32[]{:S(2)}, u32[]{:S(2)}) collective-permute-start(bf16[4,24,1024]{2,1,0:T(8,128)(2,1)S(1)} %get-tuple-element.130), channel_id=1, source_target_pairs={{0,24},{8,0},{16,8},{24,16},{1,25},{9,1},{17,9},{25,17},{2,26},{10... | collective-permute-start | bytes 589832 | tf_op jit(solution)/shard_map/ppermute | solution.py:30
  383.3 34.4 %collective-permute-start.55 = (bf16[4,4,32,1024]{3,2,0,1:T(8,128)(2,1)S(1)}, bf16[4,4,32,1024]{3,2,0,1:T(8,128)(2,1)S(1)}, u32[]{:S(2)}, u32[]{:S(2)}) collective-permute-start(bf16[4,4,32,1024]{3,2,0,1:T(8,128)(2,1)S(1)} %bitcast.223), channel_id=1, source_target_pairs={{0,16},{8,24},{16,0},{24,8},{1,17},{9,25},{17,1},{25,9},{2,18},{10... | collective-permute-start | bytes 3145736 | tf_op jit(solution)/shard_map/ppermute | solution.py:30
  385.1 48.7 %collective-permute-start.54 = (bf16[4,4,32,1024]{3,2,0,1:T(8,128)(2,1)S(1)}, bf16[4,4,32,1024]{3,2,0,1:T(8,128)(2,1)S(1)}, u32[]{:S(2)}, u32[]{:S(2)}) collective-permute-start(bf16[4,4,32,1024]{3,2,0,1:T(8,128)(2,1)S(1)} %bitcast.222), channel_id=1, source_target_pairs={{0,24},{8,0},{16,8},{24,16},{1,25},{9,1},{17,9},{25,17},{2,26},{10... | collective-permute-start | bytes 3145736 | tf_op jit(solution)/shard_map/ppermute | solution.py:30
  395.1 90.6 %collective-permute-start.24 = (f32[128,1024]{1,0:T(8,128)S(1)}, f32[128,1024]{1,0:T(8,128)}, u32[]{:S(2)}, u32[]{:S(2)}) collective-permute-start(f32[128,1024]{1,0:T(8,128)S(1)} %copy-done.10), channel_id=1, source_target_pairs={{0,1},{1,0},{2,3},{3,2},{4,5},{5,4},{6,7},{7,6},{8,9},{9,8},{10,11... | collective-permute-start | bytes 1572872 | tf_op jit(solution)/shard_map/ppermute | solution.py:34
  398.7 67.7 %collective-permute-start.31 = (bf16[4,128,1024]{2,1,0:T(8,128)(2,1)S(1)}, bf16[4,128,1024]{2,1,0:T(8,128)(2,1)S(1)}, u32[]{:S(2)}, u32[]{:S(2)}) collective-permute-start(bf16[4,128,1024]{2,1,0:T(8,128)(2,1)S(1)} %get-tuple-element.97), channel_id=1, source_target_pairs={{0,1},{1,0},{2,3},{3,2},{4,5},{5,4},{6,7},{7,6},{8,9},{9,8},{10,11... | collective-permute-start | bytes 3145736 | tf_op jit(solution)/shard_map/ppermute | solution.py:34
  398.8 37.9 %collective-permute-start.53 = (bf16[16,1536]{1,0:T(8,128)(2,1)S(1)}, bf16[16,1536]{1,0:T(8,128)(2,1)S(1)}, u32[]{:S(2)}, u32[]{:S(2)}) collective-permute-start(bf16[16,1536]{1,0:T(8,128)(2,1)S(1)} %get-tuple-element.152), channel_id=1, source_target_pairs={{0,8},{8,16},{16,24},{24,0},{1,9},{9,17},{17,25},{25,1},{2,10},{10... | collective-permute-start | bytes 147464 | tf_op jit(solution)/shard_map/ppermute | solution.py:30
  417.7 19.1 %collective-permute-start.52 = (bf16[16,1536]{1,0:T(8,128)(2,1)S(1)}, bf16[16,1536]{1,0:T(8,128)(2,1)S(1)}, u32[]{:S(2)}, u32[]{:S(2)}) collective-permute-start(bf16[16,1536]{1,0:T(8,128)(2,1)S(1)} %get-tuple-element.153), channel_id=1, source_target_pairs={{0,16},{8,24},{16,0},{24,8},{1,17},{9,25},{17,1},{25,9},{2,18},{10... | collective-permute-start | bytes 147464 | tf_op jit(solution)/shard_map/ppermute | solution.py:30
  436.7 14.3 %collective-permute-start.59 = (bf16[4,32,1024]{2,1,0:T(8,128)(2,1)S(1)}, bf16[4,32,1024]{2,1,0:T(8,128)(2,1)S(1)}, u32[]{:S(2)}, u32[]{:S(2)}) collective-permute-start(bf16[4,32,1024]{2,1,0:T(8,128)(2,1)S(1)} %get-tuple-element.125), channel_id=1, source_target_pairs={{0,2},{2,4},{4,6},{6,0},{1,3},{3,5},{5,7},{7,1},{8,10},{10,12},{12... | collective-permute-start | bytes 786440 | tf_op jit(solution)/shard_map/ppermute | solution.py:30
  436.8 14.2 %collective-permute-start.58 = (bf16[4,32,1024]{2,1,0:T(8,128)(2,1)S(1)}, bf16[4,32,1024]{2,1,0:T(8,128)(2,1)S(1)}, u32[]{:S(2)}, u32[]{:S(2)}) collective-permute-start(bf16[4,32,1024]{2,1,0:T(8,128)(2,1)S(1)} %get-tuple-element.126), channel_id=1, source_target_pairs={{0,4},{2,6},{4,0},{6,2},{1,5},{3,7},{5,1},{7,3},{8,12},{10,14},{12... | collective-permute-start | bytes 786440 | tf_op jit(solution)/shard_map/ppermute | solution.py:30
  439.6 12.4 %collective-permute-start.57 = (bf16[4,32,1024]{2,1,0:T(8,128)(2,1)S(1)}, bf16[4,32,1024]{2,1,0:T(8,128)(2,1)S(1)}, u32[]{:S(2)}, u32[]{:S(2)}) collective-permute-start(bf16[4,32,1024]{2,1,0:T(8,128)(2,1)S(1)} %get-tuple-element.124), channel_id=1, source_target_pairs={{0,6},{2,0},{4,2},{6,4},{1,7},{3,1},{5,3},{7,5},{8,14},{10,8},{12,... | collective-permute-start | bytes 786440 | tf_op jit(solution)/shard_map/ppermute | solution.py:30
  452.0 8.2 %collective-permute-start.70 = (bf16[24,1024]{1,0:T(8,128)(2,1)S(1)}, bf16[24,1024]{1,0:T(8,128)(2,1)S(1)}, u32[]{:S(2)}, u32[]{:S(2)}) collective-permute-start(bf16[24,1024]{1,0:T(8,128)(2,1)S(1)} %get-tuple-element.148), channel_id=1, source_target_pairs={{0,6},{2,0},{4,2},{6,4},{1,7},{3,1},{5,3},{7,5},{8,14},{10,8},{12,... | collective-permute-start | bytes 147464 | tf_op jit(solution)/shard_map/ppermute | solution.py:30
  467.7 15.9 %collective-permute-start.34 = (bf16[128,1024]{1,0:T(8,128)(2,1)}, bf16[128,1024]{1,0:T(8,128)(2,1)}, u32[]{:S(2)}, u32[]{:S(2)}) collective-permute-start(bf16[128,1024]{1,0:T(8,128)(2,1)} %get-tuple-element.128), channel_id=1, source_target_pairs={{0,8},{8,16},{16,24},{24,0},{1,9},{9,17},{17,25},{25,1},{2,10},{10... | collective-permute-start | bytes 786440 | tf_op jit(solution)/shard_map/ppermute | solution.py:30
  467.7 15.9 %collective-permute-start.33 = (bf16[128,1024]{1,0:T(8,128)(2,1)}, bf16[128,1024]{1,0:T(8,128)(2,1)}, u32[]{:S(2)}, u32[]{:S(2)}) collective-permute-start(bf16[128,1024]{1,0:T(8,128)(2,1)} %get-tuple-element.129), channel_id=1, source_target_pairs={{0,16},{8,24},{16,0},{24,8},{1,17},{9,25},{17,1},{25,9},{2,18},{10... | collective-permute-start | bytes 786440 | tf_op jit(solution)/shard_map/ppermute | solution.py:30
  469.4 14.7 %collective-permute-start.32 = (bf16[128,1024]{1,0:T(8,128)(2,1)}, bf16[128,1024]{1,0:T(8,128)(2,1)}, u32[]{:S(2)}, u32[]{:S(2)}) collective-permute-start(bf16[128,1024]{1,0:T(8,128)(2,1)} %get-tuple-element.127), channel_id=1, source_target_pairs={{0,24},{8,0},{16,8},{24,16},{1,25},{9,1},{17,9},{25,17},{2,26},{10... | collective-permute-start | bytes 786440 | tf_op jit(solution)/shard_map/ppermute | solution.py:30
  (69 other events, 956.3 us)
Sparse Core Ops, SparseCore 0:
  17.3 114.0 all-gather.2
